TPU v7x, 256 devices: a whole 4x4x8 slice. The times are simulated.
256 devices in a mesh: row: 16 (over x, y_hi, core), col: 16 (over z, y_lo).
Axes of the slice: x: 4, y: 4 (y_hi: 2, y_lo: 2; y = y_hi * 2 + y_lo), z: 8, core: 2. Of those that a mesh axis runs over, the one named last changes fastest.
Arguments:
- features: float32 [65536, 128], P(('row', 'col')), may hold values from -6 to 6
- weight: float32 [128, 256], replicated, may hold values from -2 to 2
- offset: float32 [256], replicated, may hold values from -3 to 3
- cotangent: float32 [65536, 256], P(('row', 'col')), may hold values from -6 to 6
- tile_index: int32 [16, 16, 2, 32], P('row', 'col'), may hold values from 0 to 15, as said below
- edge_mask: int32 [16, 16, 32, 256, 256], P('row', 'col'), may hold values from 0 to 1, as said below
Outputs:
- hidden: float32 [65536, 256], P(('row', 'col'))
- grad_features: float32 [65536, 128], P(('row', 'col'))
- grad_weight: float32 [128, 256], replicated
- grad_offset: float32 [256], replicated
Inputs may be any that keep to these rules, and one draw needn't show every extreme that they name: `tile_index`: on each device the listed tiles are distinct and come first in its slots; a device lists 32, 16, 8 or 4 tiles and at least one device lists 32; the slots after the listed ones name block 0 of both slabs. The first entry counts block rows of the row slab, the second block columns of the column slab. `edge_mask`: slots after a device's listed tiles hold only zeros.
All inputs are finite; a program needn't handle non-finite values.
Results may differ from a plain program's by a relative error of at most 0.0003.
Values sent between devices are 32-bit elements; how exact they have to be, the bound alone decides.
No kernel may reach another device: no remote copies, remote signals or barrier semaphores. Data moves between devices by JAX's collectives and lax.ppermute only.
A program may use at most 128 MiB of HBM per device.

v0:
```python
import jax
import jax.numpy as jnp
from jax import lax
from jax.sharding import PartitionSpec as P

highest = lax.Precision.HIGHEST


def gaussian_unit(values):
    return 0.5 * values * (1.0 + lax.erf(values * 0.7071067811865476))


def gaussian_slope(values):
    return (
        0.5 * (1.0 + lax.erf(values * 0.7071067811865476))
        + values * jnp.exp(-0.5 * values * values) * 0.3989422804014327
    )


def collect_blocks(slab_rows, block_ids, tile_size):
    blocks = slab_rows.reshape(slab_rows.shape[0] // tile_size, tile_size, slab_rows.shape[1])
    return jnp.take(blocks, block_ids, axis=0)


def spread_blocks(values, block_ids, block_count):
    onehot = (jnp.arange(block_count, dtype=jnp.int32)[:, None] == block_ids[None, :]).astype(
        jnp.float32
    )
    flattened = values.reshape(values.shape[0], -1)
    summed = jnp.dot(onehot, flattened, precision=highest, preferred_element_type=jnp.float32)
    return summed.reshape((block_count * values.shape[1],) + values.shape[2:])


def per_device(features, weight, offset, cotangent, tile_index, edge_mask):
    tile_size = edge_mask.shape[-1]
    group_rows = features.shape[0]
    row_count = lax.axis_size("row")
    col_count = lax.axis_size("col")
    row_blocks = col_count * group_rows // tile_size
    col_blocks = row_count * group_rows // tile_size
    tile_rows = tile_index[0, 0, 0]
    tile_cols = tile_index[0, 0, 1]
    edge_values = edge_mask[0, 0].astype(jnp.float32)
    contract_last = (((1,), (1,)), ((), ()))
    contract_first = (((0,), (0,)), ((), ()))
    moving = jnp.dot(features, weight, precision=highest, preferred_element_type=jnp.float32)
    column_slab = lax.all_gather(moving, "row", axis=0, tiled=True)
    picked = collect_blocks(column_slab, tile_cols, tile_size)
    products = jnp.einsum("tuv,tvf->tuf", edge_values, picked, precision=highest)
    partial_value = spread_blocks(products, tile_rows, row_blocks)
    edge_counts = spread_blocks(jnp.sum(edge_values, axis=2), tile_rows, row_blocks)
    summed, degree = (
        lax.psum_scatter(partial_value, "col", scatter_dimension=0, tiled=True),
        lax.psum_scatter(edge_counts, "col", scatter_dimension=0, tiled=True),
    )
    degree = 1.0 + degree
    aggregated = (summed + moving) / degree[:, None]
    activation_in = aggregated + offset
    hidden = gaussian_unit(activation_in)
    grad_pre = cotangent * gaussian_slope(activation_in)
    outgoing = grad_pre / degree[:, None]
    row_slab = lax.all_gather(outgoing, "col", axis=0, tiled=True)
    picked_back = collect_blocks(row_slab, tile_rows, tile_size)
    backward = jnp.einsum("tuv,tuf->tvf", edge_values, picked_back, precision=highest)
    partial_back = spread_blocks(backward, tile_cols, col_blocks)
    gathered = lax.psum_scatter(partial_back, "row", scatter_dimension=0, tiled=True) + outgoing
    grad_features = lax.dot_general(
        gathered, weight, contract_last, precision=highest, preferred_element_type=jnp.float32
    )
    local_weight = lax.dot_general(
        features, gathered, contract_first, precision=highest, preferred_element_type=jnp.float32
    )
    local_offset = jnp.sum(grad_pre, axis=0)
    total_weight, total_offset = lax.psum((local_weight, local_offset), ("row", "col"))
    node_total = group_rows * row_count * col_count
    factor = 1.0 / jnp.sqrt(jnp.asarray(node_total, jnp.float32))
    return (hidden, grad_features, total_weight * factor, total_offset * factor)


def solution(mesh):
    placed = (
        P(("row", "col"), None),
        P(),
        P(),
        P(("row", "col"), None),
        P("row", "col", None, None),
        P("row", "col", None, None, None),
    )
    return jax.shard_map(
        per_device,
        mesh=mesh,
        in_specs=placed,
        out_specs=(P(("row", "col"), None), P(("row", "col"), None), P(), P()),
        check_vma=False,
    )
```

profile of v0, /device:TPU:8, one launch (start us, length us, event | category | flops | bytes accessed | tf_op | source)
XLA Modules:
  0.0 725.5 jit_solution(3950802035476400927)
XLA Ops:
  8.1 2.0 fusion.38
  11.7 62.8 %all-gather.3.cloned.1.call-done = f32[4096,256]{1,0:T(8,128)} async-done(((f32[256,256]{1,0:T(8,128)}), f32[4096,256]{1,0:T(8,128)}) %all-gather.3.cloned.1.call-update) | async-done | bytes 4194320 | tf_op jit(solution)/shard_map/all_gather | solution.py:47
  74.4 6.5 gather_fusion
  80.9 23.7 %fusion.12 = f32[32,256,256]{1,2,0:T(8,128)} fusion(s32[1,1,32,256,256]{4,3,2,1,0:T(8,128)} %param.13, f32[32,256,256]{2,1,0:T(8,128)} %gather_fusion, pred[32]{0:T(512)(128)(4,1)S(1)} %get-tuple-element.27), kind=kOutput, calls=%fused_computation.15 | convolution fusion | flops 6446645248 | bytes 25165856 | tf_op jit(solution)/shard_map/tuv,tvf->tuf/dot_general | solution.py:49
  104.6 10.3 %copy.23 = f32[4,8,256,256]{3,1,2,0:T(8,128)} copy(f32[4,8,256,256]{2,3,1,0:T(8,128)} %bitcast.45) | data formatting | bytes 16777216
  114.9 8.4 %fusion.30 = f32[16,65536]{1,0:T(8,128)} fusion(f32[32,65536]{1,0:T(8,128)} %bitcast.47, s32[32]{0:T(128)S(1)} %get-tuple-element.26), kind=kOutput, calls=%fused_computation.35 | convolution fusion | flops 402653696 | bytes 12583040 | tf_op jit(solution)/shard_map/dot_general | solution.py:30
  123.3 3.8 reshape.41
  128.6 4.5 convert_reduce_fusion
  133.3 63.7 %all-reduce = f32[4096]{0:T(1024)S(1)} all-reduce(f32[4096]{0:T(1024)S(1)} %bitcast.50), channel_id=3, replica_groups=mesh['row'=16,'col'=16] {'col'}, use_global_device_ids=true, to_apply=%region_2.4.clone | all-reduce | flops 4096 | bytes 32768
  197.1 30.3 %reduce-scatter.3.cloned.1.call-done = f32[256,256]{1,0:T(8,128)} async-done(((f32[4096,256]{1,0:T(8,128)}), f32[256,256]{1,0:T(8,128)}) %reduce-scatter.3.cloned.1.call-update) | async-done | bytes 262160 | tf_op jit(solution)/shard_map/reduce_scatter | solution.py:53
  227.4 1.2 fusion.37
  228.6 0.9 broadcast_divide_fusion
  229.6 100.3 %all-gather.5.cloned.1.call-done = f32[4096,256]{1,0:T(8,128)} async-done(((f32[256,256]{1,0:T(8,128)}), f32[4096,256]{1,0:T(8,128)}) %all-gather.5.cloned.1.call-update) | async-done | bytes 4194320 | tf_op jit(solution)/shard_map/all_gather | solution.py:62
  329.9 6.5 gather_fusion.1
  336.4 21.7 %fusion.17 = f32[32,256,256]{1,2,0:T(8,128)} fusion(s32[1,1,32,256,256]{4,3,2,1,0:T(8,128)} %param.13, f32[32,256,256]{2,1,0:T(8,128)} %gather_fusion.1, pred[32]{0:T(512)(128)(4,1)S(1)} %get-tuple-element.19), kind=kOutput, calls=%fused_computation.16 | convolution fusion | flops 6446645248 | bytes 25165856 | tf_op jit(solution)/shard_map/tuv,tuf->tvf/dot_general | solution.py:64
  358.0 10.3 %copy.25 = f32[4,8,256,256]{3,1,2,0:T(8,128)} copy(f32[4,8,256,256]{2,3,1,0:T(8,128)} %bitcast.46) | data formatting | bytes 16777216
  368.3 8.4 %fusion.31 = f32[16,65536]{1,0:T(8,128)} fusion(f32[32,65536]{1,0:T(8,128)} %bitcast.44, s32[32]{0:T(128)S(1)} %get-tuple-element.25), kind=kOutput, calls=%fused_computation.36 | convolution fusion | flops 402653696 | bytes 12583040 | tf_op jit(solution)/shard_map/dot_general | solution.py:30
  376.7 3.9 reshape.45
  380.7 75.7 %psum.15 = f32[256]{0:T(256)S(1)} all-reduce(f32[256]{0:T(256)S(1)} %get-tuple-element.17), channel_id=1, replica_groups=mesh['row'=16,'col'=16] {'row','col'}, use_global_device_ids=true, to_apply=%region_6.8 | all-reduce | flops 256 | bytes 2048 | tf_op jit(solution)/shard_map/psum | solution.py:74
  457.0 11.7 %reduce-scatter.5.cloned.1.call-done = f32[256,256]{1,0:T(8,128)} async-done(((f32[4096,256]{1,0:T(8,128)}), f32[256,256]{1,0:T(8,128)}) %reduce-scatter.5.cloned.1.call-update) | async-done | bytes 262160 | tf_op jit(solution)/shard_map/reduce_scatter | solution.py:66
  468.7 2.2 convolution_bitcast_fusion
  470.9 2.0 fusion.28
  472.9 244.5 %all-reduce.3.cloned.1.call-done = f32[128,256]{0,1:T(8,128)} async-done(((f32[128,256]{0,1:T(8,128)}), f32[128,256]{0,1:T(8,128)}) %all-reduce.3.cloned.1.call-update) | async-done | bytes 131088 | tf_op jit(solution)/shard_map/psum | solution.py:74
  717.3 0.9 broadcast_multiply_fusion
  (34 shorter events, 5.0 us)
Async XLA Ops:
  7.2 0.9 copy-start
  7.2 67.2 %all-gather.3.cloned.1.call-start = ((), (), s32[]{:S(2)}) async-start(), calls=%async_computation.2 | async-start | bytes 4456448 | tf_op jit(solution)/shard_map/all_gather | solution.py:47
  10.1 217.3 %reduce-scatter.3.cloned.1.call-start = ((), (), s32[]{:S(2)}) async-start(), calls=%async_computation.3 | async-start | bytes 4456448 | tf_op jit(solution)/shard_map/reduce_scatter | solution.py:53
  123.3 4.1 copy-start.6
  127.1 100.3 %copy-start.2 = (f32[256,256]{1,0:T(8,128)S(1)}, f32[256,256]{1,0:T(8,128)}, u32[]{:S(2)}) copy-start(f32[256,256]{1,0:T(8,128)} %fusion.38) | copy-start | bytes 786436
  127.1 100.3 %copy-start.3 = (f32[256,256]{1,0:T(8,128)S(1)}, f32[256,256]{1,0:T(8,128)}, u32[]{:S(2)}) copy-start(f32[256,256]{1,0:T(8,128)} %param.11) | copy-start | bytes 786436
  127.1 100.3 %copy-start.5 = (f32[256]{0:T(256)S(1)}, f32[256]{0:T(256)}, u32[]{:S(2)}) copy-start(f32[256]{0:T(256)} %param.10) | copy-start | bytes 3076
  127.1 202.8 %all-gather.5.cloned.1.call-start = ((), (), s32[]{:S(2)}) async-start(), calls=%async_computation.4 | async-start | bytes 4456448 | tf_op jit(solution)/shard_map/all_gather | solution.py:62
  229.5 239.1 %reduce-scatter.5.cloned.1.call-start = ((), (), s32[]{:S(2)}) async-start(), calls=%async_computation.5 | async-start | bytes 4456448 | tf_op jit(solution)/shard_map/reduce_scatter | solution.py:66
  376.7 91.9 %copy-start.1 = (f32[256,256]{1,0:T(8,128)S(1)}, f32[256,256]{1,0:T(8,128)}, u32[]{:S(2)}) copy-start(f32[256,256]{1,0:T(8,128)} %get-tuple-element.23) | copy-start | bytes 786436
  376.7 94.2 %copy-start.4 = (f32[128,256]{1,0:T(8,128)S(1)}, f32[128,256]{1,0:T(8,128)}, u32[]{:S(2)}) copy-start(f32[128,256]{1,0:T(8,128)} %param.9) | copy-start | bytes 393220
  380.6 336.7 %all-reduce.3.cloned.1.call-start = ((), (), s32[]{:S(2)}) async-start(), calls=%async_computation.6 | async-start | bytes 262144 | tf_op jit(solution)/shard_map/psum | solution.py:74
Sparse Core Ops, SparseCore 0:
  11.3 63.0 all-gather.2
  127.3 100.0 reduce-scatter.2
  229.6 100.2 all-gather.4
  380.8 87.8 reduce-scatter.4
  475.5 241.8 all-reduce.2
where the time goes:
time: 726 us
  waiting for transfers between devices  450 us (62%)
  blocking collectives  139 us (19%)
  matrix products  68.4 us (9%)
  local copies, waits for them, and re-layouts  44.3 us (6%)
  between operations  14.5 us (2%)
  other arithmetic  8.97 us (1%)
    psum x1, waiting for transfers between devices, per_device(): lax.psum((local_weight, local_offset), ('row', 'col'))  244 us
    all_gather x1, waiting for transfers between devices, per_device(): row_slab = lax.all_gather(outgoing, 'col', axis=0, tiled=True)  100 us
    psum x1, blocking collectives, per_device(): lax.psum((local_weight, local_offset), ('row', 'col'))  75.7 us
    unnamed x1, blocking collectives  63.7 us
    all_gather x1, waiting for transfers between devices, per_device(): column_slab = lax.all_gather(moving, 'row', axis=0, tiled=True)  62.8 us
    reduce_scatter x1, waiting for transfers between devices, per_device(): lax.psum_scatter(partial_value, 'col', scatter_dimension=0, tiled=True)  30.3 us
    dot_general x1, matrix products, per_device(): jnp.einsum('tuv,tvf->tuf', edge_values, picked, precision=highest)  23.7 us
    unnamed x19, local copies, waits for them, and re-layouts  22.8 us
  transfers between devices with their start and end apart: 5, of which 5 were waited for; matrix products, arithmetic and copies ran while one was open for 1% of the time, Pallas kernels for 0%

commit v1 on v0

v1 whole, which is shorter than its diff:
```python
import functools

import jax
import jax.numpy as jnp
import numpy as np
from jax import lax
from jax.experimental import pallas as pl
from jax.experimental.pallas import tpu as pltpu
from jax.sharding import Mesh
from jax.sharding import PartitionSpec as P

SIZES = {"x": 4, "yh": 2, "core": 2, "z": 8, "yl": 2}
AXES = tuple(SIZES)
F = 128
H = 256
TILE = 256
TMAX = 32
BLOCKS = 16
COUNT = 8
BLOCK = F + COUNT
PIECE = 16
STEP = 4
highest = lax.Precision.HIGHEST
f32 = jnp.float32
bf16 = jnp.bfloat16


def shift(value, axis, by):
    size = SIZES[axis]
    return lax.ppermute(value, axis, [(i, (i + by) % size) for i in range(size)])


def whole(shape):
    return pl.BlockSpec(shape, lambda *_: (0,) * len(shape))


def params(mib):
    return pltpu.CompilerParams(vmem_limit_bytes=mib * 1024 * 1024)


def split_terms(values):
    high = values.astype(bf16)
    return high, (values - high.astype(f32)).astype(bf16)


def narrow_body(mask_ref, out_ref):
    out_ref[...] = mask_ref[...].astype(f32).astype(bf16)


def narrow_mask(mask):
    spec = pl.BlockSpec((STEP, TILE, TILE), lambda t: (t, 0, 0))
    return pl.pallas_call(
        narrow_body,
        grid=(TMAX // STEP,),
        in_specs=[spec],
        out_specs=spec,
        out_shape=jax.ShapeDtypeStruct((TMAX, TILE, TILE), bf16),
        compiler_params=params(16),
        cost_estimate=pl.CostEstimate(
            flops=TMAX * TILE * TILE, bytes_accessed=6 * TMAX * TILE * TILE, transcendentals=0
        ),
    )(mask)


def source_slot(block):
    x, yh, core = block >> 2, (block >> 1) & 1, block & 1
    x_rel = (x - lax.axis_index("x")) & 3
    yh_rel = yh ^ lax.axis_index("yh")
    core_rel = core ^ lax.axis_index("core")
    return core_rel * 8 + x_rel * 2 + yh_rel


def target_slot(block):
    z, yl = block >> 1, block & 1
    return ((z - lax.axis_index("z")) & 7) * 2 + (yl ^ lax.axis_index("yl"))


def forward_body(index_ref, mask_ref, *refs):
    sources, (out_ref, held) = refs[:16], refs[16:]
    step = pl.program_id(0)

    @pl.when(step == 0)
    def _():
        for slot in range(BLOCKS):
            high, low = split_terms(sources[slot][...])
            held[slot, :F, :] = high
            held[slot, F : 2 * F, :] = low
            held[slot, 2 * F :, :] = jnp.ones((16, TILE), bf16)
        out_ref[...] = jnp.zeros_like(out_ref)

    for k in range(STEP):
        tile = step * STEP + k
        target = target_slot(index_ref[0, tile])
        source = source_slot(index_ref[1, tile])
        product = lax.dot_general(
            held[source], mask_ref[k], (((1,), (1,)), ((), ())), preferred_element_type=f32
        )
        out_ref[target, :F, :] += product[:F] + product[F : 2 * F]
        out_ref[target, F:, :] += product[2 * F : 2 * F + COUNT]


def forward_products(index, mask, sources):
    return pl.pallas_call(
        forward_body,
        grid=(TMAX // STEP,),
        in_specs=[
            pl.BlockSpec(memory_space=pltpu.SMEM),
            pl.BlockSpec((STEP, TILE, TILE), lambda t: (t, 0, 0)),
        ]
        + [whole((F, TILE))] * BLOCKS,
        out_specs=whole((BLOCKS, BLOCK, TILE)),
        out_shape=jax.ShapeDtypeStruct((BLOCKS, BLOCK, TILE), f32),
        scratch_shapes=[pltpu.VMEM((BLOCKS, 2 * F + 16, TILE), bf16)],
        compiler_params=params(32),
        cost_estimate=pl.CostEstimate(
            flops=4 * TMAX * TILE * TILE * F, bytes_accessed=2 * TMAX * TILE * TILE, transcendentals=0
        ),
    )(index, mask, *sources)


def dense_body(a_ref, b_ref, c_ref, d_ref, x_ref, w_ref, o_ref, g_ref, hidden_ref, out_ref, gw_ref):
    total = a_ref[...] + b_ref[...] + c_ref[...] + d_ref[...]
    degree = 1.0 + total[F : F + 1]
    aggregated = (total[:F] + x_ref[...]) / degree
    weight = w_ref[...]
    active = (
        jnp.dot(aggregated.T, weight, precision=highest, preferred_element_type=f32) + o_ref[...]
    )
    bell = 1.0 + lax.erf(active * 0.7071067811865476)
    hidden_ref[...] = 0.5 * active * bell
    slope = 0.5 * bell + active * jnp.exp(-0.5 * active * active) * 0.3989422804014327
    grad_pre = g_ref[...] * slope
    out_ref[...] = (
        lax.dot_general(
            weight, grad_pre, (((1,), (1,)), ((), ())), precision=highest, preferred_element_type=f32
        )
        / degree
    )
    grad_weight = jnp.dot(aggregated, grad_pre, precision=highest, preferred_element_type=f32)
    offset = jnp.broadcast_to(jnp.sum(grad_pre, axis=0, keepdims=True), (8, H))
    for k in range(BLOCKS):
        gw_ref[k, :8, :] = grad_weight[8 * k : 8 * k + 8]
        gw_ref[k, 8:, :] = offset


def dense(parts, x_t, weight, offset, cotangent):
    return pl.pallas_call(
        dense_body,
        out_shape=(
            jax.ShapeDtypeStruct((TILE, H), f32),
            jax.ShapeDtypeStruct((F, TILE), f32),
            jax.ShapeDtypeStruct((BLOCKS, PIECE, H), f32),
        ),
        compiler_params=params(32),
    )(*parts, x_t, weight, offset.reshape(1, H), cotangent)


def backward_body(index_ref, mask_ref, *refs):
    ins, (near_ref, far_ref, held, sums) = refs[:9], refs[9:]
    step = pl.program_id(0)
    places = [(0, 0), (7, 1), (1, 2), (6, 3), (2, 4), (5, 5), (3, 6)]
    parts = [(2 * z + h, ins[k], h * (F + PIECE)) for z, k in places for h in range(2)]
    parts += [(8, ins[7], 0), (9, ins[8], 0)]

    @pl.when(step == 0)
    def _():
        for slot, ref, start in parts:
            high, low = split_terms(ref[start : start + F, :])
            held[slot, :F, :] = high
            held[slot, F:, :] = low
        sums[...] = jnp.zeros_like(sums)

    for k in range(STEP):
        tile = step * STEP + k
        source = target_slot(index_ref[0, tile])
        target = source_slot(index_ref[1, tile])
        product = jnp.dot(held[source], mask_ref[k], preferred_element_type=f32)
        sums[target] += product[:F] + product[F:]

    @pl.when(step == TMAX // STEP - 1)
    def _():
        piece = jnp.zeros((PIECE, H), f32)
        for slot, ref, start in parts:
            piece = piece + ref[start + F : start + F + PIECE, :]
        for slot in range(8):
            near_ref[slot * F : (slot + 1) * F, :] = sums[slot]
            far_ref[slot * F : (slot + 1) * F, :] = sums[8 + slot]
        near_ref[8 * F :, :] = piece
        far_ref[8 * F :, :] = piece


def backward_products(index, mask, gathered):
    rows = 8 * F + PIECE
    return pl.pallas_call(
        backward_body,
        grid=(TMAX // STEP,),
        in_specs=[
            pl.BlockSpec(memory_space=pltpu.SMEM),
            pl.BlockSpec((STEP, TILE, TILE), lambda t: (t, 0, 0)),
        ]
        + [whole(value.shape) for value in gathered],
        out_specs=(whole((rows, TILE)), whole((rows, TILE))),
        out_shape=(jax.ShapeDtypeStruct((rows, TILE), f32),) * 2,
        scratch_shapes=[
            pltpu.VMEM((BLOCKS, 2 * F, TILE), bf16),
            pltpu.VMEM((BLOCKS, F, TILE), f32),
        ],
        compiler_params=params(32),
        cost_estimate=pl.CostEstimate(
            flops=4 * TMAX * TILE * TILE * F, bytes_accessed=2 * TMAX * TILE * TILE, transcendentals=0
        ),
    )(index, mask, *gathered)


def final_body(scale, near_ref, other_ref, out_ref, pieces_ref, yonder_ref, grad_ref, gw_ref, go_ref):
    grad_ref[...] = (near_ref[...] + other_ref[:F, :] + out_ref[...]).T
    x, yh, core = (lax.axis_index(a) for a in ("x", "yh", "core"))
    for h, ref, start in ((0, pieces_ref, 0), (1, yonder_ref, F)):
        for k, by in enumerate((0, 3, 1, 2)):
            for c in range(2):
                block = ((x + by) & 3) * 4 + (yh ^ h) * 2 + (core ^ c)
                at = start + (k * 2 + c) * PIECE
                gw_ref[pl.ds(pl.multiple_of(block * 8, 8), 8), :] = ref[at : at + 8, :] * scale
    go_ref[...] = pieces_ref[8:16, :] * scale


def finish(near, other, outgoing, pieces, scale):
    return pl.pallas_call(
        functools.partial(final_body, scale),
        out_shape=(
            jax.ShapeDtypeStruct((TILE, F), f32),
            jax.ShapeDtypeStruct((F, H), f32),
            jax.ShapeDtypeStruct((8, H), f32),
        ),
        compiler_params=params(16),
    )(near, other, outgoing, pieces, other)


def gather_row(x_t):
    h = shift(x_t, "yh", 1)
    r1, l1 = shift(x_t, "x", 1), shift(x_t, "x", -1)
    r1h, l1h = shift(h, "x", 1), shift(h, "x", -1)
    r2, l2 = shift(r1, "x", 1), shift(l1h, "x", -1)
    own = [x_t, h, l1, l1h, r2, l2, r1, r1h]
    pairs = [[x_t, h], [l1, r1], [l1h, r1h], [r2, l2]]
    far = []
    for a, b in pairs:
        both = shift(jnp.concatenate([a, b], axis=0), "core", 1)
        far.append((both[:F], both[F:]))
    (f0, f1), (f2, f6), (f3, f7), (f4, f5) = far
    return own + [f0, f1, f2, f3, f4, f5, f6, f7]


def scatter_col(sums):
    two = lambda z: sums[2 * (z % 8) : 2 * (z % 8) + 2].reshape(2 * BLOCK, TILE)
    right, left = shift(sums[8], "z", 1), shift(sums[9], "z", -1)
    right = two(3).at[:BLOCK].add(right)
    left = two(-3).at[BLOCK:].add(left)
    right, left = shift(right, "z", 1), shift(left, "z", -1)
    right, left = shift(right + two(2), "z", 1), shift(left + two(-2), "z", -1)
    right, left = shift(right + two(1), "z", 1), shift(left + two(-1), "z", -1)
    other = shift(right[BLOCK:] + left[BLOCK:] + sums[1], "yl", 1)
    return sums[0], right[:BLOCK], left[:BLOCK], other


def gather_col(value):
    half = value.shape[0]
    both = jnp.concatenate([value, shift(value, "yl", 1)], axis=0)
    r1, l1 = shift(both, "z", 1), shift(both, "z", -1)
    r2, l2 = shift(r1, "z", 1), shift(l1, "z", -1)
    r3, l3 = shift(r2, "z", 1), shift(l2, "z", -1)
    r4, l4 = shift(r3[:half], "z", 1), shift(l3[half:], "z", -1)
    return both, r1, l1, r2, l2, r3, l3, r4, l4


def scatter_row(near, far):
    got = shift(far, "core", 1)
    total = near[: 8 * F] + got[: 8 * F]
    pieces = jnp.concatenate([near[8 * F :], got[8 * F :]], axis=0)
    two = lambda x: total[x % 4 * 2 * F : (x % 4 * 2 + 2) * F]
    right = shift(jnp.concatenate([two(2)[:F], pieces], axis=0), "x", 1)
    left = shift(jnp.concatenate([two(2)[F:], pieces], axis=0), "x", -1)
    from_left, from_right = right[F:], left[F:]
    right = jnp.concatenate([two(1).at[:F].add(right[:F]), from_left], axis=0)
    left = two(-1).at[F:].add(left[:F])
    right, left = shift(right, "x", 1), shift(left, "x", -1)
    mine = two(0) + right[: 2 * F] + left
    pieces = jnp.concatenate([pieces, from_left, from_right, right[2 * F :]], axis=0)
    other = shift(jnp.concatenate([mine[F:], pieces], axis=0), "yh", 1)
    return mine[:F], other, pieces


def per_device(features, weight, offset, cotangent, tile_index, edge_mask):
    index = tile_index.reshape(2, TMAX)
    x_t = features.T
    sources = gather_row(x_t)
    mask = narrow_mask(edge_mask.reshape(TMAX, TILE, TILE))
    sums = forward_products(index, mask, sources)
    parts = scatter_col(sums)
    hidden, outgoing, gw = dense(parts, x_t, weight, offset, cotangent)
    spread = lax.all_to_all(gw, ("x", "yh", "core"), 0, 0, tiled=True)
    piece = jnp.sum(spread, axis=0)
    gathered = gather_col(jnp.concatenate([outgoing, piece], axis=0))
    near, far = backward_products(index, mask, gathered)
    mine, other, pieces = scatter_row(near, far)
    scale = 1.0 / float(np.sqrt(BLOCKS * BLOCKS * TILE))
    grad, grad_weight, grad_offset = finish(mine, other, outgoing, pieces, scale)
    return hidden, grad, grad_weight, grad_offset[0]


def solution(mesh):
    fine = Mesh(mesh.devices.reshape(tuple(SIZES.values())), AXES)
    row, col = ("x", "yh", "core"), ("z", "yl")
    nodes = P(row + col, None)
    return jax.shard_map(
        per_device,
        mesh=fine,
        in_specs=(
            nodes,
            P(),
            P(),
            nodes,
            P(row, col, None, None),
            P(row, col, None, None, None),
        ),
        out_specs=(nodes, nodes, P(), P()),
        check_vma=False,
    )
```

time: 726 us -> 168 us (0.23)
  waiting for transfers between devices: 450 us -> 86.1 us
  blocking collectives: 139 us -> 13.6 us
  matrix products: 68.4 us -> 0 us
  starting transfers between devices: 0.39 us -> 46.7 us
  local copies, waits for them, and re-layouts: 44.3 us -> 7.49 us
  between operations: 14.5 us -> 1.05 us
  Pallas kernels: 0 us -> 10.6 us
  other arithmetic: 8.97 us -> 0.64 us
    psum x1 -> x0, waiting for transfers between devices: 244 us -> none  [per_device(): lax.psum((local_weight, local_offset), ('row', 'col'))]
    all_gather x2 -> x0, waiting for transfers between devices: 163 us -> none  [the longest x1 100 us: per_device(): row_slab = lax.all_gather(outgoing, 'col', axis=0, tiled=True)]
    ppermute x0 -> x35, waiting for transfers between devices: none -> 86.1 us  [shift(): lax.ppermute(value, axis, [(i, (i + by) % size) for i in range(size)])]
    psum x1 -> x0, blocking collectives: 75.7 us -> none  [per_device(): lax.psum((local_weight, local_offset), ('row', 'col'))]
    dot_general x8 -> x0, matrix products: 68.4 us -> none  [the longest x1 23.7 us: per_device(): jnp.einsum('tuv,tvf->tuf', edge_values, picked, precision=highest)]
    unnamed x1 -> x0, blocking collectives: 63.7 us -> none
    ppermute x0 -> x35, starting transfers between devices: none -> 46.7 us  [shift(): lax.ppermute(value, axis, [(i, (i + by) % size) for i in range(size)])]
    reduce_scatter x2 -> x0, waiting for transfers between devices: 42 us -> none  [the longest x1 30.3 us: per_device(): lax.psum_scatter(partial_value, 'col', scatter_dimension=0, tiled=True)]
  transfers between devices with their start and end apart: 5 -> 35, of which waited for: 5 -> 23; matrix products, arithmetic and copies ran while one was open for 1% -> 0% of each run, Pallas kernels for 0% -> 0%
where the time goes in v1:
time: 168 us; the launch traced here: 166 us
  waiting for transfers between devices  86.1 us (51%)
  starting transfers between devices  46.7 us (28%)
  blocking collectives  13.6 us (8%)
  Pallas kernels  10.6 us (6%)
  local copies, waits for them, and re-layouts  7.49 us (4%)
    ppermute x35, waiting for transfers between devices, shift(): lax.ppermute(value, axis, [(i, (i + by) % size) for i in range(size)])  86.1 us
    ppermute x35, starting transfers between devices, shift(): lax.ppermute(value, axis, [(i, (i + by) % size) for i in range(size)])  46.7 us
    all_to_all x1, blocking collectives, per_device(): spread = lax.all_to_all(gw, ('x', 'yh', 'core'), 0, 0, tiled=True)  13.6 us
    unnamed x20, local copies, waits for them, and re-layouts  6.63 us
    pallas_call x1, Pallas kernels, forward_products(): pl.pallas_call(forward_body, grid=(TMAX // STEP,), in_specs=[pl.BlockSpec...  3.95 us
    pallas_call x1, Pallas kernels, backward_products(): pl.pallas_call(backward_body, grid=(TMAX // STEP,), in_specs=[pl.BlockSpe...  3.77 us
  transfers between devices with their start and end apart: 35, of which 23 were waited for; matrix products, arithmetic and copies ran while one was open for 0% of the time, Pallas kernels for 0%

profile of v1, /device:TPU:8, one launch (start us, length us, event | category | flops | bytes accessed | tf_op | source)
XLA Modules:
  0.0 166.3 jit_solution(6632931348364019793)
XLA Ops:
  11.2 3.4 %copy-done.2 = s32[1,1,32,256,256]{4,3,2,1,0:T(8,128)S(1)} copy-done((s32[1,1,32,256,256]{4,3,2,1,0:T(8,128)S(1)}, s32[1,1,32,256,256]{4,3,2,1,0:T(8,128)}, u32[]{:S(2)}) %copy-start.2) | copy-done | bytes 8388632
  18.9 3.8 %collective-permute-done.6.refs_7_ = f32[128,256]{1,0:T(8,128)S(1)} collective-permute-done((f32[128,256]{1,0:T(8,128)S(1)}, f32[128,256]{1,0:T(8,128)S(1)}, u32[]{:S(2)}, u32[]{:S(2)}) %collective-permute-start.6) | collective-permute-done | bytes 131104 | tf_op jit(solution)/shard_map/ppermute | solution.py:30
  25.8 3.9 %shard_map.94 = f32[16,136,256]{2,1,0:T(8,128)S(1)} custom-call(s32[2,32]{1,0:T(2,128)S(1)} %bitcast.44, bf16[32,256,256]{2,1,0:T(8,128)(2,1)S(1)} %shard_map.93.mask_ref, f32[128,256]{1,0:T(8,128)S(1)} %bitcast.42, f32[128,256]{1,0:T(8,128)S(1)} %collective-permute-done.refs_1_, f32[128,256]{1,0:T(8,128)S(1)} %collective-permute-done.1.refs_2_, ...), custom_call_target="tpu_custom_call" | custom-call | flops 1073741824 | bytes 4194304 | tf_op jit(solution)/shard_map/pallas_call | solution.py:103
  29.8 5.9 %collective-permute-start.15 = (f32[136,256]{1,0:T(8,128)S(1)}, f32[136,256]{1,0:T(8,128)S(1)}, u32[]{:S(2)}, u32[]{:S(2)}) collective-permute-start(f32[136,256]{1,0:T(8,128)S(1)} %get-tuple-element.76), channel_id=1, source_target_pairs={{0,14},{2,0},{4,2},{6,4},{8,6},{10,8},{12,10},{14,12},{1,15},{3,1}... | collective-permute-start | bytes 417800 | tf_op jit(solution)/shard_map/ppermute | solution.py:30
  35.9 3.1 %collective-permute-done.15 = f32[136,256]{1,0:T(8,128)S(1)} collective-permute-done((f32[136,256]{1,0:T(8,128)S(1)}, f32[136,256]{1,0:T(8,128)S(1)}, u32[]{:S(2)}, u32[]{:S(2)}) %collective-permute-start.15) | collective-permute-done | bytes 139296 | tf_op jit(solution)/shard_map/ppermute | solution.py:30
  39.0 3.4 %collective-permute-done.11 = f32[136,256]{1,0:T(8,128)S(1)} collective-permute-done((f32[136,256]{1,0:T(8,128)S(1)}, f32[136,256]{1,0:T(8,128)S(1)}, u32[]{:S(2)}, u32[]{:S(2)}) %collective-permute-start.11) | collective-permute-done | bytes 139296 | tf_op jit(solution)/shard_map/ppermute | solution.py:30
  44.6 5.5 %collective-permute-done.16 = f32[272,256]{1,0:T(8,128)S(1)} collective-permute-done((f32[272,256]{1,0:T(8,128)S(1)}, f32[272,256]{1,0:T(8,128)S(1)}, u32[]{:S(2)}, u32[]{:S(2)}) %collective-permute-start.16) | collective-permute-done | bytes 278560 | tf_op jit(solution)/shard_map/ppermute | solution.py:30
  52.5 4.6 %collective-permute-done.17 = f32[272,256]{1,0:T(8,128)S(1)} collective-permute-done((f32[272,256]{1,0:T(8,128)S(1)}, f32[272,256]{1,0:T(8,128)S(1)}, u32[]{:S(2)}, u32[]{:S(2)}) %collective-permute-start.17) | collective-permute-done | bytes 278560 | tf_op jit(solution)/shard_map/ppermute | solution.py:30
  57.1 3.3 %collective-permute-start.18 = (f32[272,256]{1,0:T(8,128)S(1)}, f32[272,256]{1,0:T(8,128)S(1)}, u32[]{:S(2)}, u32[]{:S(2)}) collective-permute-start(f32[272,256]{1,0:T(8,128)S(1)} %bitcast_add_fusion), channel_id=1, source_target_pairs={{0,14},{2,0},{4,2},{6,4},{8,6},{10,8},{12,10},{14,12},{1,15},{3,1}... | collective-permute-start | bytes 835592 | tf_op jit(solution)/shard_map/ppermute | solution.py:30
  60.6 3.9 %collective-permute-done.18 = f32[272,256]{1,0:T(8,128)S(1)} collective-permute-done((f32[272,256]{1,0:T(8,128)S(1)}, f32[272,256]{1,0:T(8,128)S(1)}, u32[]{:S(2)}, u32[]{:S(2)}) %collective-permute-start.18) | collective-permute-done | bytes 278560 | tf_op jit(solution)/shard_map/ppermute | solution.py:30
  64.6 3.8 %collective-permute-done.14 = f32[272,256]{1,0:T(8,128)S(1)} collective-permute-done((f32[272,256]{1,0:T(8,128)S(1)}, f32[272,256]{1,0:T(8,128)S(1)}, u32[]{:S(2)}, u32[]{:S(2)}) %collective-permute-start.14) | collective-permute-done | bytes 278560 | tf_op jit(solution)/shard_map/ppermute | solution.py:30
  68.9 4.6 %collective-permute-done.19.d_ref = f32[136,256]{1,0:T(8,128)S(1)} collective-permute-done((f32[136,256]{1,0:T(8,128)S(1)}, f32[136,256]{1,0:T(8,128)S(1)}, u32[]{:S(2)}, u32[]{:S(2)}) %collective-permute-start.19) | collective-permute-done | bytes 139296 | tf_op jit(solution)/shard_map/ppermute | solution.py:30
  75.2 13.6 %all_to_all.5 = f32[16,16,256]{2,1,0:T(8,128)S(1)} all-to-all(f32[16,16,256]{2,1,0:T(8,128)S(1)} %get-tuple-element.62), channel_id=1, replica_groups=mesh['x'=4,'yh'=2,'core'=2,'z'=8,'yl'=2] {'x','yh','core'}, dimensions={0} | all-to-all | bytes 524288 | tf_op jit(solution)/shard_map/all_to_all | solution.py:301
  90.4 4.5 %collective-permute-done.20 = f32[144,256]{1,0:T(8,128)S(1)} collective-permute-done((f32[144,256]{1,0:T(8,128)S(1)}, f32[144,256]{1,0:T(8,128)S(1)}, u32[]{:S(2)}, u32[]{:S(2)}) %collective-permute-start.20) | collective-permute-done | bytes 147488 | tf_op jit(solution)/shard_map/ppermute | solution.py:30
  97.0 6.2 %collective-permute-done.22.refs_2_ = f32[288,256]{1,0:T(8,128)S(1)} collective-permute-done((f32[288,256]{1,0:T(8,128)S(1)}, f32[288,256]{1,0:T(8,128)S(1)}, u32[]{:S(2)}, u32[]{:S(2)}) %collective-permute-start.22) | collective-permute-done | bytes 294944 | tf_op jit(solution)/shard_map/ppermute | solution.py:30
  105.2 5.2 %collective-permute-done.24.refs_4_ = f32[288,256]{1,0:T(8,128)S(1)} collective-permute-done((f32[288,256]{1,0:T(8,128)S(1)}, f32[288,256]{1,0:T(8,128)S(1)}, u32[]{:S(2)}, u32[]{:S(2)}) %collective-permute-start.24) | collective-permute-done | bytes 294944 | tf_op jit(solution)/shard_map/ppermute | solution.py:30
  110.4 3.0 %collective-permute-start.26 = (f32[288,256]{1,0:T(8,128)S(1)}, f32[288,256]{1,0:T(8,128)S(1)}, u32[]{:S(2)}, u32[]{:S(2)}) collective-permute-start(f32[288,256]{1,0:T(8,128)S(1)} %collective-permute-done.24.refs_4_), channel_id=1, source_target_pairs={{0,14},{2,0},{4,2},{6,4},{8,6},{10,8},{12,10},{14,12},{1,15},{3,1}... | collective-permute-start | bytes 884744 | tf_op jit(solution)/shard_map/ppermute | solution.py:30
  113.4 4.2 %collective-permute-done.26.refs_6_ = f32[288,256]{1,0:T(8,128)S(1)} collective-permute-done((f32[288,256]{1,0:T(8,128)S(1)}, f32[288,256]{1,0:T(8,128)S(1)}, u32[]{:S(2)}, u32[]{:S(2)}) %collective-permute-start.26) | collective-permute-done | bytes 294944 | tf_op jit(solution)/shard_map/ppermute | solution.py:30
  117.7 3.8 %collective-permute-start.28 = (f32[144,256]{1,0:T(8,128)S(1)}, f32[144,256]{1,0:T(8,128)S(1)}, u32[]{:S(2)}, u32[]{:S(2)}) collective-permute-start(f32[144,256]{1,0:T(8,128)S(1)} %slice.283), channel_id=1, source_target_pairs={{0,14},{2,0},{4,2},{6,4},{8,6},{10,8},{12,10},{14,12},{1,15},{3,1}... | collective-permute-start | bytes 442376 | tf_op jit(solution)/shard_map/ppermute | solution.py:30
  124.1 3.8 %collective-permute-done.27.refs_7_ = f32[144,256]{1,0:T(8,128)S(1)} collective-permute-done((f32[144,256]{1,0:T(8,128)S(1)}, f32[144,256]{1,0:T(8,128)S(1)}, u32[]{:S(2)}, u32[]{:S(2)}) %collective-permute-start.27) | collective-permute-done | bytes 147488 | tf_op jit(solution)/shard_map/ppermute | solution.py:30
  130.1 3.8 %shard_map.96 = (f32[1040,256]{1,0:T(8,128)S(1)}, f32[1040,256]{1,0:T(8,128)S(1)}) custom-call(s32[2,32]{1,0:T(2,128)S(1)} %bitcast.45, bf16[32,256,256]{2,1,0:T(8,128)(2,1)S(1)} %copy-done.1, f32[288,256]{1,0:T(8,128)S(1)} %pad_maximum_fusion.refs_0_, f32[288,256]{1,0:T(8,128)S(1)} %collective-permute-done.21.refs_1_, ...), custom_call_target="tpu_custom_call" | custom-call | flops 1073741824 | bytes 4194304 | tf_op jit(solution)/shard_map/pallas_call | solution.py:194
  139.1 5.4 %collective-permute-done.30 = f32[160,256]{1,0:T(8,128)S(1)} collective-permute-done((f32[160,256]{1,0:T(8,128)S(1)}, f32[160,256]{1,0:T(8,128)S(1)}, u32[]{:S(2)}, u32[]{:S(2)}) %collective-permute-start.30) | collective-permute-done | bytes 163872 | tf_op jit(solution)/shard_map/ppermute | solution.py:30
  146.8 3.3 %collective-permute-done.32 = f32[160,256]{1,0:T(8,128)S(1)} collective-permute-done((f32[160,256]{1,0:T(8,128)S(1)}, f32[160,256]{1,0:T(8,128)S(1)}, u32[]{:S(2)}, u32[]{:S(2)}) %collective-permute-start.32) | collective-permute-done | bytes 163872 | tf_op jit(solution)/shard_map/ppermute | solution.py:30
  158.6 6.4 %collective-permute-done.34.other_ref.yonder_ref = f32[256,256]{1,0:T(8,128)S(1)} collective-permute-done((f32[256,256]{1,0:T(8,128)S(1)}, f32[256,256]{1,0:T(8,128)S(1)}, u32[]{:S(2)}, u32[]{:S(2)}) %collective-permute-start.34) | collective-permute-done | bytes 262176 | tf_op jit(solution)/shard_map/ppermute | solution.py:30
  (107 shorter events, 52.6 us)
Async XLA Ops:
  1.6 6.8 %collective-permute-start = (f32[128,256]{1,0:T(8,128)S(1)}, f32[128,256]{1,0:T(8,128)S(1)}, u32[]{:S(2)}, u32[]{:S(2)}) collective-permute-start(f32[128,256]{1,0:T(8,128)S(1)} %bitcast.38), channel_id=1, source_target_pairs={{0,32},{32,0},{1,33},{33,1},{2,34},{34,2},{3,35},{35,3},{4,36},{36... | collective-permute-start | bytes 393224 | tf_op jit(solution)/shard_map/ppermute | solution.py:30
  4.0 11.2 %collective-permute-start.3 = (f32[128,256]{1,0:T(8,128)S(1)}, f32[128,256]{1,0:T(8,128)S(1)}, u32[]{:S(2)}, u32[]{:S(2)}) collective-permute-start(f32[128,256]{1,0:T(8,128)S(1)} %bitcast.39), channel_id=1, source_target_pairs={{0,64},{64,128},{128,192},{192,0},{1,65},{65,129},{129,193},{193,1... | collective-permute-start | bytes 393224 | tf_op jit(solution)/shard_map/ppermute | solution.py:30
  5.5 9.7 %collective-permute-start.1 = (f32[128,256]{1,0:T(8,128)S(1)}, f32[128,256]{1,0:T(8,128)S(1)}, u32[]{:S(2)}, u32[]{:S(2)}) collective-permute-start(f32[128,256]{1,0:T(8,128)S(1)} %bitcast.40), channel_id=1, source_target_pairs={{0,192},{64,0},{128,64},{192,128},{1,193},{65,1},{129,65},{193,129... | collective-permute-start | bytes 393224 | tf_op jit(solution)/shard_map/ppermute | solution.py:30
  8.5 7.7 %collective-permute-start.2 = (f32[128,256]{1,0:T(8,128)S(1)}, f32[128,256]{1,0:T(8,128)S(1)}, u32[]{:S(2)}, u32[]{:S(2)}) collective-permute-start(f32[128,256]{1,0:T(8,128)S(1)} %collective-permute-done.refs_1_), channel_id=1, source_target_pairs={{0,192},{64,0},{128,64},{192,128},{1,193},{65,1},{129,65},{193,129... | collective-permute-start | bytes 393224 | tf_op jit(solution)/shard_map/ppermute | solution.py:30
  15.1 7.6 %collective-permute-start.6 = (f32[128,256]{1,0:T(8,128)S(1)}, f32[128,256]{1,0:T(8,128)S(1)}, u32[]{:S(2)}, u32[]{:S(2)}) collective-permute-start(f32[128,256]{1,0:T(8,128)S(1)} %collective-permute-done.refs_1_), channel_id=1, source_target_pairs={{0,64},{64,128},{128,192},{192,0},{1,65},{65,129},{129,193},{193,1... | collective-permute-start | bytes 393224 | tf_op jit(solution)/shard_map/ppermute | solution.py:30
  15.3 9.0 %collective-permute-start.8 = (f32[256,256]{1,0:T(8,128)S(1)}, f32[256,256]{1,0:T(8,128)S(1)}, u32[]{:S(2)}, u32[]{:S(2)}) collective-permute-start(f32[256,256]{1,0:T(8,128)S(1)} %pad_maximum_fusion.3), channel_id=1, source_target_pairs={{0,16},{16,0},{1,17},{17,1},{2,18},{18,2},{3,19},{19,3},{4,20},{20... | collective-permute-start | bytes 786440 | tf_op jit(solution)/shard_map/ppermute | solution.py:30
  15.4 8.8 %collective-permute-start.4 = (f32[128,256]{1,0:T(8,128)S(1)}, f32[128,256]{1,0:T(8,128)S(1)}, u32[]{:S(2)}, u32[]{:S(2)}) collective-permute-start(f32[128,256]{1,0:T(8,128)S(1)} %collective-permute-done.3.refs_6_), channel_id=1, source_target_pairs={{0,64},{64,128},{128,192},{192,0},{1,65},{65,129},{129,193},{193,1... | collective-permute-start | bytes 393224 | tf_op jit(solution)/shard_map/ppermute | solution.py:30
  16.2 8.0 %collective-permute-start.5 = (f32[128,256]{1,0:T(8,128)S(1)}, f32[128,256]{1,0:T(8,128)S(1)}, u32[]{:S(2)}, u32[]{:S(2)}) collective-permute-start(f32[128,256]{1,0:T(8,128)S(1)} %collective-permute-done.2.refs_3_), channel_id=1, source_target_pairs={{0,192},{64,0},{128,64},{192,128},{1,193},{65,1},{129,65},{193,129... | collective-permute-start | bytes 393224 | tf_op jit(solution)/shard_map/ppermute | solution.py:30
  29.8 9.2 %collective-permute-start.15 = (f32[136,256]{1,0:T(8,128)S(1)}, f32[136,256]{1,0:T(8,128)S(1)}, u32[]{:S(2)}, u32[]{:S(2)}) collective-permute-start(f32[136,256]{1,0:T(8,128)S(1)} %get-tuple-element.76), channel_id=1, source_target_pairs={{0,14},{2,0},{4,2},{6,4},{8,6},{10,8},{12,10},{14,12},{1,15},{3,1}... | collective-permute-start | bytes 417800 | tf_op jit(solution)/shard_map/ppermute | solution.py:30
  42.5 7.6 %collective-permute-start.16 = (f32[272,256]{1,0:T(8,128)S(1)}, f32[272,256]{1,0:T(8,128)S(1)}, u32[]{:S(2)}, u32[]{:S(2)}) collective-permute-start(f32[272,256]{1,0:T(8,128)S(1)} %get-tuple-element.74), channel_id=1, source_target_pairs={{0,14},{2,0},{4,2},{6,4},{8,6},{10,8},{12,10},{14,12},{1,15},{3,1}... | collective-permute-start | bytes 835592 | tf_op jit(solution)/shard_map/ppermute | solution.py:30
  42.8 9.4 %collective-permute-start.12 = (f32[272,256]{1,0:T(8,128)S(1)}, f32[272,256]{1,0:T(8,128)S(1)}, u32[]{:S(2)}, u32[]{:S(2)}) collective-permute-start(f32[272,256]{1,0:T(8,128)S(1)} %get-tuple-element.75), channel_id=1, source_target_pairs={{0,2},{2,4},{4,6},{6,8},{8,10},{10,12},{12,14},{14,0},{1,3},{3,5},... | collective-permute-start | bytes 835592 | tf_op jit(solution)/shard_map/ppermute | solution.py:30
  50.1 7.0 %collective-permute-start.17 = (f32[272,256]{1,0:T(8,128)S(1)}, f32[272,256]{1,0:T(8,128)S(1)}, u32[]{:S(2)}, u32[]{:S(2)}) collective-permute-start(f32[272,256]{1,0:T(8,128)S(1)} %bitcast_add_fusion.1), channel_id=1, source_target_pairs={{0,14},{2,0},{4,2},{6,4},{8,6},{10,8},{12,10},{14,12},{1,15},{3,1}... | collective-permute-start | bytes 835592 | tf_op jit(solution)/shard_map/ppermute | solution.py:30
  52.3 8.2 %collective-permute-start.13 = (f32[272,256]{1,0:T(8,128)S(1)}, f32[272,256]{1,0:T(8,128)S(1)}, u32[]{:S(2)}, u32[]{:S(2)}) collective-permute-start(f32[272,256]{1,0:T(8,128)S(1)} %bitcast_add_fusion.3), channel_id=1, source_target_pairs={{0,2},{2,4},{4,6},{6,8},{8,10},{10,12},{12,14},{14,0},{1,3},{3,5},... | collective-permute-start | bytes 835592 | tf_op jit(solution)/shard_map/ppermute | solution.py:30
  57.1 7.4 %collective-permute-start.18 = (f32[272,256]{1,0:T(8,128)S(1)}, f32[272,256]{1,0:T(8,128)S(1)}, u32[]{:S(2)}, u32[]{:S(2)}) collective-permute-start(f32[272,256]{1,0:T(8,128)S(1)} %bitcast_add_fusion), channel_id=1, source_target_pairs={{0,14},{2,0},{4,2},{6,4},{8,6},{10,8},{12,10},{14,12},{1,15},{3,1}... | collective-permute-start | bytes 835592 | tf_op jit(solution)/shard_map/ppermute | solution.py:30
  60.5 7.8 %collective-permute-start.14 = (f32[272,256]{1,0:T(8,128)S(1)}, f32[272,256]{1,0:T(8,128)S(1)}, u32[]{:S(2)}, u32[]{:S(2)}) collective-permute-start(f32[272,256]{1,0:T(8,128)S(1)} %bitcast_add_fusion.2), channel_id=1, source_target_pairs={{0,2},{2,4},{4,6},{6,8},{8,10},{10,12},{12,14},{14,0},{1,3},{3,5},... | collective-permute-start | bytes 835592 | tf_op jit(solution)/shard_map/ppermute | solution.py:30
  94.9 8.3 %collective-permute-start.22 = (f32[288,256]{1,0:T(8,128)S(1)}, f32[288,256]{1,0:T(8,128)S(1)}, u32[]{:S(2)}, u32[]{:S(2)}) collective-permute-start(f32[288,256]{1,0:T(8,128)S(1)} %pad_maximum_fusion.refs_0_), channel_id=1, source_target_pairs={{0,14},{2,0},{4,2},{6,4},{8,6},{10,8},{12,10},{14,12},{1,15},{3,1}... | collective-permute-start | bytes 884744 | tf_op jit(solution)/shard_map/ppermute | solution.py:30
  95.0 9.7 %collective-permute-start.21 = (f32[288,256]{1,0:T(8,128)S(1)}, f32[288,256]{1,0:T(8,128)S(1)}, u32[]{:S(2)}, u32[]{:S(2)}) collective-permute-start(f32[288,256]{1,0:T(8,128)S(1)} %pad_maximum_fusion.refs_0_), channel_id=1, source_target_pairs={{0,2},{2,4},{4,6},{6,8},{8,10},{10,12},{12,14},{14,0},{1,3},{3,5},... | collective-permute-start | bytes 884744 | tf_op jit(solution)/shard_map/ppermute | solution.py:30
  103.2 7.3 %collective-permute-start.24 = (f32[288,256]{1,0:T(8,128)S(1)}, f32[288,256]{1,0:T(8,128)S(1)}, u32[]{:S(2)}, u32[]{:S(2)}) collective-permute-start(f32[288,256]{1,0:T(8,128)S(1)} %collective-permute-done.22.refs_2_), channel_id=1, source_target_pairs={{0,14},{2,0},{4,2},{6,4},{8,6},{10,8},{12,10},{14,12},{1,15},{3,1}... | collective-permute-start | bytes 884744 | tf_op jit(solution)/shard_map/ppermute | solution.py:30
  104.7 8.8 %collective-permute-start.23 = (f32[288,256]{1,0:T(8,128)S(1)}, f32[288,256]{1,0:T(8,128)S(1)}, u32[]{:S(2)}, u32[]{:S(2)}) collective-permute-start(f32[288,256]{1,0:T(8,128)S(1)} %collective-permute-done.21.refs_1_), channel_id=1, source_target_pairs={{0,2},{2,4},{4,6},{6,8},{8,10},{10,12},{12,14},{14,0},{1,3},{3,5},... | collective-permute-start | bytes 884744 | tf_op jit(solution)/shard_map/ppermute | solution.py:30
  110.4 7.2 %collective-permute-start.26 = (f32[288,256]{1,0:T(8,128)S(1)}, f32[288,256]{1,0:T(8,128)S(1)}, u32[]{:S(2)}, u32[]{:S(2)}) collective-permute-start(f32[288,256]{1,0:T(8,128)S(1)} %collective-permute-done.24.refs_4_), channel_id=1, source_target_pairs={{0,14},{2,0},{4,2},{6,4},{8,6},{10,8},{12,10},{14,12},{1,15},{3,1}... | collective-permute-start | bytes 884744 | tf_op jit(solution)/shard_map/ppermute | solution.py:30
  113.4 8.0 %collective-permute-start.25 = (f32[288,256]{1,0:T(8,128)S(1)}, f32[288,256]{1,0:T(8,128)S(1)}, u32[]{:S(2)}, u32[]{:S(2)}) collective-permute-start(f32[288,256]{1,0:T(8,128)S(1)} %collective-permute-done.23.refs_3_), channel_id=1, source_target_pairs={{0,2},{2,4},{4,6},{6,8},{8,10},{10,12},{12,14},{14,0},{1,3},{3,5},... | collective-permute-start | bytes 884744 | tf_op jit(solution)/shard_map/ppermute | solution.py:30
  137.0 7.5 %collective-permute-start.30 = (f32[160,256]{1,0:T(8,128)S(1)}, f32[160,256]{1,0:T(8,128)S(1)}, u32[]{:S(2)}, u32[]{:S(2)}) collective-permute-start(f32[160,256]{1,0:T(8,128)S(1)} %pad_maximum_fusion.7), channel_id=1, source_target_pairs={{0,64},{64,128},{128,192},{192,0},{1,65},{65,129},{129,193},{193,1... | collective-permute-start | bytes 491528 | tf_op jit(solution)/shard_map/ppermute | solution.py:30
  144.8 9.5 %collective-permute-start.31 = (f32[288,256]{1,0:T(8,128)S(1)}, f32[288,256]{1,0:T(8,128)S(1)}, u32[]{:S(2)}, u32[]{:S(2)}) collective-permute-start(f32[288,256]{1,0:T(8,128)S(1)} %pad_maximum_fusion.1), channel_id=1, source_target_pairs={{0,64},{64,128},{128,192},{192,0},{1,65},{65,129},{129,193},{193,1... | collective-permute-start | bytes 884744 | tf_op jit(solution)/shard_map/ppermute | solution.py:30
  157.0 8.0 %collective-permute-start.34 = (f32[256,256]{1,0:T(8,128)S(1)}, f32[256,256]{1,0:T(8,128)S(1)}, u32[]{:S(2)}, u32[]{:S(2)}) collective-permute-start(f32[256,256]{1,0:T(8,128)S(1)} %get-tuple-element.88), channel_id=1, source_target_pairs={{0,32},{32,0},{1,33},{33,1},{2,34},{34,2},{3,35},{35,3},{4,36},{36... | collective-permute-start | bytes 786440 | tf_op jit(solution)/shard_map/ppermute | solution.py:30
  (18 other events, 155.9 us)

commit v2 on v1

v2 whole, which is shorter than its diff:
```python
import jax
import jax.numpy as jnp
import numpy as np
from jax import lax
from jax.experimental import pallas as pl
from jax.experimental.pallas import tpu as pltpu
from jax.sharding import Mesh
from jax.sharding import PartitionSpec as P

SIZES = {"x": 4, "yh": 2, "core": 2, "z": 8, "yl": 2}
AXES = tuple(SIZES)
PLANE = ("x", "yh")
F = 128
H = 256
TILE = 256
TMAX = 32
BLOCKS = 16
COUNT = 8
BLOCK = F + COUNT
SHARE = 16
PIECE = SHARE + 8
CUTS = (0, 8, 16, TMAX)
PARTS = len(CUTS) - 1
highest = lax.Precision.HIGHEST
f32 = jnp.float32
bf16 = jnp.bfloat16
together = lax.optimization_barrier


def shift(value, axis, by):
    size = SIZES[axis]
    return lax.ppermute(value, axis, [(i, (i + by) % size) for i in range(size)])


def params(mib):
    return pltpu.CompilerParams(vmem_limit_bytes=mib * 1024 * 1024)


def cost(tiles):
    return pl.CostEstimate(
        flops=4 * tiles * TILE * TILE * F, bytes_accessed=2 * TMAX * TILE * TILE, transcendentals=0
    )


def split_terms(values):
    high = values.astype(bf16)
    return high, (values - high.astype(f32)).astype(bf16)


def source_slot(block):
    x, yh, core = block >> 2, (block >> 1) & 1, block & 1
    x_rel = (x - lax.axis_index("x")) & 3
    yh_rel = yh ^ lax.axis_index("yh")
    core_rel = core ^ lax.axis_index("core")
    return core_rel * 8 + x_rel * 2 + yh_rel


def target_slot(block):
    z, yl = block >> 1, block & 1
    return ((z - lax.axis_index("z")) & 7) * 2 + (yl ^ lax.axis_index("yl"))


def over_tiles(mask_refs, use):
    for start, ref in zip(CUTS, mask_refs):
        for k in range(ref.shape[0]):
            use(start + k, ref[k].astype(f32).astype(bf16))


def forward_body(index_ref, *refs):
    masks, sources, (out_ref, held) = refs[:PARTS], refs[PARTS:-2], refs[-2:]
    for slot in range(BLOCKS):
        high, low = split_terms(sources[slot][...])
        held[slot, :F, :] = high
        held[slot, F : 2 * F, :] = low
        held[slot, 2 * F :, :] = jnp.ones((16, TILE), bf16)
    out_ref[...] = jnp.zeros_like(out_ref)

    def use(tile, mask):
        target = target_slot(index_ref[0, tile])
        source = source_slot(index_ref[1, tile])
        product = lax.dot_general(
            held[source], mask, (((1,), (1,)), ((), ())), preferred_element_type=f32
        )
        out_ref[target, :F, :] += product[:F] + product[F : 2 * F]
        out_ref[target, F:, :] += product[2 * F : 2 * F + COUNT]

    over_tiles(masks, use)


def vmem(count):
    return [pl.BlockSpec(memory_space=pltpu.SMEM)] + [pl.BlockSpec(memory_space=pltpu.VMEM)] * count


def forward_products(index, masks, sources):
    return pl.pallas_call(
        forward_body,
        in_specs=vmem(PARTS + BLOCKS),
        out_shape=jax.ShapeDtypeStruct((BLOCKS, BLOCK, TILE), f32),
        scratch_shapes=[pltpu.VMEM((BLOCKS, 2 * F + 16, TILE), bf16)],
        compiler_params=params(24),
        cost_estimate=cost(TMAX),
    )(index, *masks, *sources)


def dense_body(a_ref, b_ref, c_ref, d_ref, x_ref, w_ref, o_ref, g_ref, hidden_ref, out_ref, gw_ref):
    total = a_ref[...] + b_ref[...] + c_ref[...] + d_ref[...]
    degree = 1.0 + total[F : F + 1]
    aggregated = (total[:F] + x_ref[...]) / degree
    weight = w_ref[...]
    active = (
        jnp.dot(aggregated.T, weight, precision=highest, preferred_element_type=f32) + o_ref[...]
    )
    bell = 1.0 + lax.erf(active * 0.7071067811865476)
    hidden_ref[...] = 0.5 * active * bell
    slope = 0.5 * bell + active * jnp.exp(-0.5 * active * active) * 0.3989422804014327
    grad_pre = g_ref[...] * slope
    out_ref[...] = (
        lax.dot_general(
            weight, grad_pre, (((1,), (1,)), ((), ())), precision=highest, preferred_element_type=f32
        )
        / degree
    )
    gw_ref[:F, :] = jnp.dot(aggregated, grad_pre, precision=highest, preferred_element_type=f32)
    gw_ref[F:, :] = jnp.broadcast_to(jnp.sum(grad_pre, axis=0, keepdims=True), (8, H))


def dense(parts, x_t, weight, offset, cotangent):
    return pl.pallas_call(
        dense_body,
        out_shape=(
            jax.ShapeDtypeStruct((TILE, H), f32),
            jax.ShapeDtypeStruct((F, TILE), f32),
            jax.ShapeDtypeStruct((F + 8, H), f32),
        ),
        compiler_params=params(24),
    )(*parts, x_t, weight, offset.reshape(1, H), cotangent)


def backward_body(index_ref, *refs):
    masks, ins, (near_ref, far_ref, held, sums) = refs[:PARTS], refs[PARTS:-4], refs[-4:]
    places = [(0, 0), (7, 1), (1, 2), (6, 3), (2, 4), (5, 5), (3, 6)]
    parts = [(2 * z + h, ins[k], h * F) for z, k in places for h in range(2)]
    parts += [(8, ins[7], 0), (9, ins[8], 0)]
    for slot, ref, start in parts:
        high, low = split_terms(ref[start : start + F, :])
        held[slot, :F, :] = high
        held[slot, F:, :] = low
    sums[...] = jnp.zeros_like(sums)
    core = lax.axis_index("core")

    def use(tile, mask):
        source = target_slot(index_ref[0, tile])
        block = index_ref[1, tile]
        product = jnp.dot(held[source], mask, preferred_element_type=f32)
        sums[((block & 1) ^ core) * 8 + (block >> 1)] += product[:F] + product[F:]

    over_tiles(masks, use)
    near_ref[...] = sums[:8]
    far_ref[...] = sums[8:]


def backward_products(index, masks, gathered):
    half = jax.ShapeDtypeStruct((8, F, TILE), f32)
    return pl.pallas_call(
        backward_body,
        in_specs=vmem(PARTS + len(gathered)),
        out_shape=(half, half),
        scratch_shapes=[
            pltpu.VMEM((BLOCKS, 2 * F, TILE), bf16),
            pltpu.VMEM((BLOCKS, F, TILE), f32),
        ],
        compiler_params=params(24),
        cost_estimate=cost(TMAX),
    )(index, *masks, *gathered)


SCALE = 1.0 / float(np.sqrt(BLOCKS * BLOCKS * TILE))


def final_body(parts_ref, out_ref, piece_ref, grad_ref, gw_ref, go_ref):
    total = out_ref[...]
    for k in range(8):
        total = total + parts_ref[k, :F, :]
        gw_ref[k * SHARE : (k + 1) * SHARE, :] = parts_ref[k, F:, :] * SCALE
    grad_ref[...] = total.T
    go_ref[...] = piece_ref[SHARE : SHARE + 1, :] * SCALE


def finish(parts, outgoing, piece):
    return pl.pallas_call(
        final_body,
        out_shape=(
            jax.ShapeDtypeStruct((TILE, F), f32),
            jax.ShapeDtypeStruct((F, H), f32),
            jax.ShapeDtypeStruct((1, H), f32),
        ),
        compiler_params=params(16),
    )(parts, outgoing, piece)


def gather_row(x_t, mask):
    h = shift(x_t, "yh", 1)
    r1, l1 = shift(x_t, "x", 1), shift(x_t, "x", -1)
    narrow = lambda whole, k: whole[CUTS[k] : CUTS[k + 1]].astype(jnp.int8)
    m0 = narrow(mask, 0)
    h, m0, mask = together((h, m0, mask))
    r1h, l1h = shift(h, "x", 1), shift(h, "x", -1)
    m1 = narrow(mask, 1)
    l1h, m1, mask = together((l1h, m1, mask))
    r2, l2 = shift(r1, "x", 1), shift(l1h, "x", -1)
    l2, m2 = together((l2, narrow(mask, 2)))
    own = [x_t, h, l1, l1h, r2, l2, r1, r1h]
    pairs = [[x_t, h], [l1, r1], [l1h, r1h], [r2, l2]]
    far = []
    for a, b in pairs:
        both = shift(jnp.concatenate([a, b], axis=0), "core", 1)
        far.append((both[:F], both[F:]))
    (f0, f1), (f2, f6), (f3, f7), (f4, f5) = far
    return own + [f0, f1, f2, f3, f4, f5, f6, f7], (m0, m1, m2)


def scatter_col(sums):
    two = lambda z: sums[2 * (z % 8) : 2 * (z % 8) + 2].reshape(2 * BLOCK, TILE)
    right, left = shift(sums[8], "z", 1), shift(sums[9], "z", -1)
    right = two(3).at[:BLOCK].add(right)
    left = two(-3).at[BLOCK:].add(left)
    right, left = shift(right, "z", 1), shift(left, "z", -1)
    right, left = shift(right + two(2), "z", 1), shift(left + two(-2), "z", -1)
    right, left = shift(right + two(1), "z", 1), shift(left + two(-1), "z", -1)
    other = shift(right[BLOCK:] + left[BLOCK:] + sums[1], "yl", 1)
    return sums[0], right[:BLOCK], left[:BLOCK], other


def gather_col(value, gw):
    other, gw = together((shift(value, "yl", 1), gw + shift(gw, "core", 1)))
    both = jnp.concatenate([value, other], axis=0)
    shares = jnp.concatenate(
        [gw[:F].reshape(8, SHARE, H), jnp.broadcast_to(gw[F:], (8, 8, H))], axis=1
    )
    r1, l1, shares = together(
        (
            shift(both, "z", 1),
            shift(both, "z", -1),
            lax.all_to_all(shares, PLANE, 0, 0, tiled=True),
        )
    )
    piece = jnp.sum(shares, axis=0)
    r2 = shift(jnp.concatenate([r1, piece], axis=0), "z", 1)
    l2 = shift(jnp.concatenate([l1, piece], axis=0), "z", -1)
    r3, l3 = shift(r2, "z", 1), shift(l2, "z", -1)
    r4 = shift(jnp.concatenate([r3[:F], r3[2 * F :]], axis=0), "z", 1)
    l4 = shift(l3[F:], "z", -1)
    for ref, at in ((r2, 2 * F), (l2, 2 * F), (r3, 2 * F), (l3, 2 * F), (r4, F), (l4, F)):
        piece = piece + ref[at:]
    return (both, r1, l1, r2, l2, r3, l3, r4, l4), piece, r4[F:]


def scatter_row(index, masks, gathered, piece, last):
    (near, far), last = together((backward_products(index, masks, gathered), shift(last, "z", 1)))
    piece = piece + last
    got, piece = together((shift(far, "core", 1), piece + shift(piece, "yl", 1)))
    share = jnp.broadcast_to(piece[:SHARE], (8, SHARE, H))
    total = jnp.concatenate([near + got, share], axis=1)
    return lax.all_to_all(total, PLANE, 0, 0, tiled=True), piece


def per_device(features, weight, offset, cotangent, tile_index, edge_mask):
    index = tile_index.reshape(2, TMAX)
    x_t = features.T
    sources, masks = gather_row(x_t, edge_mask.reshape(TMAX, TILE, TILE))
    parts = scatter_col(forward_products(index, masks, sources))
    hidden, outgoing, gw = dense(parts, x_t, weight, offset, cotangent)
    gathered, piece, last = gather_col(outgoing, gw)
    parts, piece = scatter_row(index, masks, gathered, piece, last)
    grad, grad_weight, grad_offset = finish(parts, outgoing, piece)
    return hidden, grad, grad_weight, grad_offset.reshape(H)


def solution(mesh):
    fine = Mesh(mesh.devices.reshape(tuple(SIZES.values())), AXES)
    row, col = ("x", "yh", "core"), ("z", "yl")
    nodes = P(row + col, None)
    return jax.shard_map(
        per_device,
        mesh=fine,
        in_specs=(
            nodes,
            P(),
            P(),
            nodes,
            P(row, col, None, None),
            P(row, col, None, None, None),
        ),
        out_specs=(nodes, nodes, P(), P()),
        check_vma=False,
    )
```

time: 168 us -> 149 us (0.89); the launches traced: 166 us -> 149 us
  waiting for transfers between devices: 86.1 us -> 56.6 us
  blocking collectives: 13.6 us -> 33.8 us
  other arithmetic: 0.64 us -> 7.4 us
  local copies, waits for them, and re-layouts: 7.49 us -> 1.32 us
  starting transfers between devices: 46.7 us -> 41.9 us
  Pallas kernels: 10.6 us -> 7.17 us
    ppermute x35 -> x33, waiting for transfers between devices: 86.1 us -> 56.6 us  [shift(): lax.ppermute(value, axis, [(i, (i + by) % size) for i in range(size)])]
    all_to_all x1 -> x2, blocking collectives: 13.6 us -> 33.8 us  [the longest x1 20.6 us: scatter_row(): return (lax.all_to_all(total, PLANE, 0, 0, tiled=True), piece)]
    unnamed x20 -> x10, local copies, waits for them, and re-layouts: 6.63 us -> 1.03 us
    another operation x0 -> x2, other arithmetic: none -> 4.92 us
    ppermute x35 -> x33, starting transfers between devices: 46.7 us -> 41.9 us  [shift(): lax.ppermute(value, axis, [(i, (i + by) % size) for i in range(size)])]
    pallas_call x4 -> x3, Pallas kernels: 8.99 us -> 5.51 us  [the longest x1 2.36 us: backward_products(): pl.pallas_call(backward_body, in_specs=vmem(PARTS + len(gathered)), out_s...]
    convert_element_type x0 -> x1, other arithmetic: none -> 1.76 us  [gather_row(): narrow = lambda whole, k: whole[CUTS[k]:CUTS[k + 1]].astype(jnp.int8)]
  transfers between devices with their start and end apart: 35 -> 33, of which waited for: 23 -> 17; matrix products, arithmetic and copies ran while one was open for 0% -> 5% of each run, Pallas kernels for 0% -> 2%
where the time goes in v2:
time: 149 us
  waiting for transfers between devices  56.6 us (38%)
  starting transfers between devices  41.9 us (28%)
  blocking collectives  33.8 us (23%)
  other arithmetic  7.4 us (5%)
  Pallas kernels  7.17 us (5%)
    ppermute x33, waiting for transfers between devices, shift(): lax.ppermute(value, axis, [(i, (i + by) % size) for i in range(size)])  56.6 us
    ppermute x33, starting transfers between devices, shift(): lax.ppermute(value, axis, [(i, (i + by) % size) for i in range(size)])  41.9 us
    all_to_all x1, blocking collectives, scatter_row(): return (lax.all_to_all(total, PLANE, 0, 0, tiled=True), piece)  20.6 us
    all_to_all x1, blocking collectives, gather_col(): lax.all_to_all(shares, PLANE, 0, 0, tiled=True)  13.2 us
    another operation x2, other arithmetic  4.92 us
  transfers between devices with their start and end apart: 33, of which 17 were waited for; matrix products, arithmetic and copies ran while one was open for 5% of the time, Pallas kernels for 2%

profile of v2, /device:TPU:8, one launch (start us, length us, event | category | flops | bytes accessed | tf_op | source)
XLA Modules:
  0.0 149.2 jit_solution(4593105974968142260)
XLA Ops:
  9.0 2.4 %collective-permute-done.refs_4_ = f32[128,256]{1,0:T(8,128)S(1)} collective-permute-done((f32[128,256]{1,0:T(8,128)S(1)}, f32[128,256]{1,0:T(8,128)S(1)}, u32[]{:S(2)}, u32[]{:S(2)}) %collective-permute-start) | collective-permute-done | bytes 131104 | tf_op jit(solution)/shard_map/ppermute | solution.py:32
  11.7 3.0 %collective-permute-start.1 = (f32[128,256]{1,0:T(8,128)S(1)}, f32[128,256]{1,0:T(8,128)S(1)}, u32[]{:S(2)}, u32[]{:S(2)}) collective-permute-start(f32[128,256]{1,0:T(8,128)S(1)} %collective-permute-done.refs_4_), channel_id=1, source_target_pairs={{0,192},{64,0},{128,64},{192,128},{1,193},{65,1},{129,65},{193,129... | collective-permute-start | bytes 393224 | tf_op jit(solution)/shard_map/ppermute | solution.py:32
  17.4 3.5 %collective-permute-start.2 = (f32[128,256]{1,0:T(8,128)S(1)}, f32[128,256]{1,0:T(8,128)S(1)}, u32[]{:S(2)}, u32[]{:S(2)}) collective-permute-start(f32[128,256]{1,0:T(8,128)S(1)} %collective-permute-done.1.refs_6_), channel_id=1, source_target_pairs={{0,192},{64,0},{128,64},{192,128},{1,193},{65,1},{129,65},{193,129... | collective-permute-start | bytes 393224 | tf_op jit(solution)/shard_map/ppermute | solution.py:32
  21.0 3.0 %slice_convert_fusion.refs_2_ = s8[16,256,256]{2,1,0:T(32,128)(4,1)S(1)} fusion(s32[32,256,256]{2,1,0:T(8,128)} %bitcast.50), kind=kLoop, calls=%fused_computation | loop fusion | flops 1048576 | bytes 5242880 | tf_op jit(solution)/shard_map/convert
  28.2 6.0 %collective-permute-start.15 = (f32[136,256]{1,0:T(8,128)S(1)}, f32[136,256]{1,0:T(8,128)S(1)}, u32[]{:S(2)}, u32[]{:S(2)}) collective-permute-start(f32[136,256]{1,0:T(8,128)S(1)} %get-tuple-element.88), channel_id=1, source_target_pairs={{0,14},{2,0},{4,2},{6,4},{8,6},{10,8},{12,10},{14,12},{1,15},{3,1}... | collective-permute-start | bytes 417800 | tf_op jit(solution)/shard_map/ppermute | solution.py:32
  34.3 3.3 %collective-permute-done.15 = f32[136,256]{1,0:T(8,128)S(1)} collective-permute-done((f32[136,256]{1,0:T(8,128)S(1)}, f32[136,256]{1,0:T(8,128)S(1)}, u32[]{:S(2)}, u32[]{:S(2)}) %collective-permute-start.15) | collective-permute-done | bytes 139296 | tf_op jit(solution)/shard_map/ppermute | solution.py:32
  37.6 3.4 %collective-permute-done.11 = f32[136,256]{1,0:T(8,128)S(1)} collective-permute-done((f32[136,256]{1,0:T(8,128)S(1)}, f32[136,256]{1,0:T(8,128)S(1)}, u32[]{:S(2)}, u32[]{:S(2)}) %collective-permute-start.11) | collective-permute-done | bytes 139296 | tf_op jit(solution)/shard_map/ppermute | solution.py:32
  43.2 5.8 %collective-permute-done.16 = f32[272,256]{1,0:T(8,128)S(1)} collective-permute-done((f32[272,256]{1,0:T(8,128)S(1)}, f32[272,256]{1,0:T(8,128)S(1)}, u32[]{:S(2)}, u32[]{:S(2)}) %collective-permute-start.16) | collective-permute-done | bytes 278560 | tf_op jit(solution)/shard_map/ppermute | solution.py:32
  51.2 4.7 %collective-permute-done.17 = f32[272,256]{1,0:T(8,128)S(1)} collective-permute-done((f32[272,256]{1,0:T(8,128)S(1)}, f32[272,256]{1,0:T(8,128)S(1)}, u32[]{:S(2)}, u32[]{:S(2)}) %collective-permute-start.17) | collective-permute-done | bytes 278560 | tf_op jit(solution)/shard_map/ppermute | solution.py:32
  56.0 3.4 %collective-permute-start.18 = (f32[272,256]{1,0:T(8,128)S(1)}, f32[272,256]{1,0:T(8,128)S(1)}, u32[]{:S(2)}, u32[]{:S(2)}) collective-permute-start(f32[272,256]{1,0:T(8,128)S(1)} %bitcast_add_fusion), channel_id=1, source_target_pairs={{0,14},{2,0},{4,2},{6,4},{8,6},{10,8},{12,10},{14,12},{1,15},{3,1}... | collective-permute-start | bytes 835592 | tf_op jit(solution)/shard_map/ppermute | solution.py:32
  59.6 3.9 %collective-permute-done.18 = f32[272,256]{1,0:T(8,128)S(1)} collective-permute-done((f32[272,256]{1,0:T(8,128)S(1)}, f32[272,256]{1,0:T(8,128)S(1)}, u32[]{:S(2)}, u32[]{:S(2)}) %collective-permute-start.18) | collective-permute-done | bytes 278560 | tf_op jit(solution)/shard_map/ppermute | solution.py:32
  63.5 3.8 %collective-permute-done.14 = f32[272,256]{1,0:T(8,128)S(1)} collective-permute-done((f32[272,256]{1,0:T(8,128)S(1)}, f32[272,256]{1,0:T(8,128)S(1)}, u32[]{:S(2)}, u32[]{:S(2)}) %collective-permute-start.14) | collective-permute-done | bytes 278560 | tf_op jit(solution)/shard_map/ppermute | solution.py:32
  67.9 4.6 %collective-permute-done.19.d_ref = f32[136,256]{1,0:T(8,128)S(1)} collective-permute-done((f32[136,256]{1,0:T(8,128)S(1)}, f32[136,256]{1,0:T(8,128)S(1)}, u32[]{:S(2)}, u32[]{:S(2)}) %collective-permute-start.19) | collective-permute-done | bytes 139296 | tf_op jit(solution)/shard_map/ppermute | solution.py:32
  75.5 4.5 %collective-permute-done.20 = f32[128,256]{1,0:T(8,128)S(1)} collective-permute-done((f32[128,256]{1,0:T(8,128)S(1)}, f32[128,256]{1,0:T(8,128)S(1)}, u32[]{:S(2)}, u32[]{:S(2)}) %collective-permute-start.20) | collective-permute-done | bytes 131104 | tf_op jit(solution)/shard_map/ppermute | solution.py:32
  82.2 13.2 %all_to_all.10 = f32[8,24,256]{2,1,0:T(8,128)S(1)} all-to-all(f32[8,24,256]{2,1,0:T(8,128)S(1)} %pad_maximum_fusion.7), channel_id=1, replica_groups=mesh['x'=4,'yh'=2,'core'=2,'z'=8,'yl'=2] {'x','yh'}, dimensions={0} | all-to-all | bytes 393216 | tf_op jit(solution)/shard_map/all_to_all | solution.py:244
  95.6 3.2 %collective-permute-start.25 = (f32[280,256]{1,0:T(8,128)S(1)}, f32[280,256]{1,0:T(8,128)S(1)}, u32[]{:S(2)}, u32[]{:S(2)}) collective-permute-start(f32[280,256]{1,0:T(8,128)S(1)} %get-tuple-element.102), channel_id=1, source_target_pairs={{0,14},{2,0},{4,2},{6,4},{8,6},{10,8},{12,10},{14,12},{1,15},{3,1}... | collective-permute-start | bytes 860168 | tf_op jit(solution)/shard_map/ppermute | solution.py:32
  98.8 4.6 %collective-permute-done.24.refs_6_ = f32[280,256]{1,0:T(8,128)S(1)} collective-permute-done((f32[280,256]{1,0:T(8,128)S(1)}, f32[280,256]{1,0:T(8,128)S(1)}, u32[]{:S(2)}, u32[]{:S(2)}) %collective-permute-start.24) | collective-permute-done | bytes 286752 | tf_op jit(solution)/shard_map/ppermute | solution.py:32
  103.4 3.2 %collective-permute-start.27 = (f32[280,256]{1,0:T(8,128)S(1)}, f32[280,256]{1,0:T(8,128)S(1)}, u32[]{:S(2)}, u32[]{:S(2)}) collective-permute-start(f32[280,256]{1,0:T(8,128)S(1)} %collective-permute-done.25.refs_7_), channel_id=1, source_target_pairs={{0,14},{2,0},{4,2},{6,4},{8,6},{10,8},{12,10},{14,12},{1,15},{3,1}... | collective-permute-start | bytes 860168 | tf_op jit(solution)/shard_map/ppermute | solution.py:32
  106.6 5.2 %collective-permute-done.26.refs_8_ = f32[280,256]{1,0:T(8,128)S(1)} collective-permute-done((f32[280,256]{1,0:T(8,128)S(1)}, f32[280,256]{1,0:T(8,128)S(1)}, u32[]{:S(2)}, u32[]{:S(2)}) %collective-permute-start.26) | collective-permute-done | bytes 286752 | tf_op jit(solution)/shard_map/ppermute | solution.py:32
  112.0 3.4 %collective-permute-start.29 = (f32[152,256]{1,0:T(8,128)S(1)}, f32[152,256]{1,0:T(8,128)S(1)}, u32[]{:S(2)}, u32[]{:S(2)}) collective-permute-start(f32[152,256]{1,0:T(8,128)S(1)} %slice.223), channel_id=1, source_target_pairs={{0,14},{2,0},{4,2},{6,4},{8,6},{10,8},{12,10},{14,12},{1,15},{3,1}... | collective-permute-start | bytes 466952 | tf_op jit(solution)/shard_map/ppermute | solution.py:32
  115.3 3.1 %collective-permute-done.28.refs_10_ = f32[152,256]{1,0:T(8,128)S(1)} collective-permute-done((f32[152,256]{1,0:T(8,128)S(1)}, f32[152,256]{1,0:T(8,128)S(1)}, u32[]{:S(2)}, u32[]{:S(2)}) %collective-permute-start.28) | collective-permute-done | bytes 155680 | tf_op jit(solution)/shard_map/ppermute | solution.py:32
  120.9 2.7 %collective-permute-done.30 = f32[24,256]{1,0:T(8,128)S(1)} collective-permute-done((f32[24,256]{1,0:T(8,128)S(1)}, f32[24,256]{1,0:T(8,128)S(1)}, u32[]{:S(2)}, u32[]{:S(2)}) %collective-permute-start.30) | collective-permute-done | bytes 24608 | tf_op jit(solution)/shard_map/ppermute | solution.py:32
  125.0 2.5 %collective-permute-done.32 = f32[24,256]{1,0:T(8,128)S(1)} collective-permute-done((f32[24,256]{1,0:T(8,128)S(1)}, f32[24,256]{1,0:T(8,128)S(1)}, u32[]{:S(2)}, u32[]{:S(2)}) %collective-permute-start.32) | collective-permute-done | bytes 24608 | tf_op jit(solution)/shard_map/ppermute | solution.py:32
  127.7 20.6 %all_to_all.11.parts_ref = f32[8,144,256]{2,1,0:T(8,128)S(1)} all-to-all(f32[8,144,256]{2,1,0:T(8,128)S(1)} %pad_maximum_fusion), channel_id=1, replica_groups=mesh['x'=4,'yh'=2,'core'=2,'z'=8,'yl'=2] {'x','yh'}, dimensions={0} | all-to-all | bytes 2359296 | tf_op jit(solution)/shard_map/all_to_all | solution.py:264
  (96 shorter events, 31.2 us)
Async XLA Ops:
  1.6 13.0 %collective-permute-start.4 = (f32[128,256]{1,0:T(8,128)S(1)}, f32[128,256]{1,0:T(8,128)S(1)}, u32[]{:S(2)}, u32[]{:S(2)}) collective-permute-start(f32[128,256]{1,0:T(8,128)S(1)} %bitcast.40), channel_id=1, source_target_pairs={{0,64},{64,128},{128,192},{192,0},{1,65},{65,129},{129,193},{193,1... | collective-permute-start | bytes 393224 | tf_op jit(solution)/shard_map/ppermute | solution.py:32
  3.2 11.5 %collective-permute-start.3 = (f32[128,256]{1,0:T(8,128)S(1)}, f32[128,256]{1,0:T(8,128)S(1)}, u32[]{:S(2)}, u32[]{:S(2)}) collective-permute-start(f32[128,256]{1,0:T(8,128)S(1)} %bitcast.41), channel_id=1, source_target_pairs={{0,192},{64,0},{128,64},{192,128},{1,193},{65,1},{129,65},{193,129... | collective-permute-start | bytes 393224 | tf_op jit(solution)/shard_map/ppermute | solution.py:32
  5.0 6.5 %collective-permute-start = (f32[128,256]{1,0:T(8,128)S(1)}, f32[128,256]{1,0:T(8,128)S(1)}, u32[]{:S(2)}, u32[]{:S(2)}) collective-permute-start(f32[128,256]{1,0:T(8,128)S(1)} %bitcast.42), channel_id=1, source_target_pairs={{0,32},{32,0},{1,33},{33,1},{2,34},{34,2},{3,35},{35,3},{4,36},{36... | collective-permute-start | bytes 393224 | tf_op jit(solution)/shard_map/ppermute | solution.py:32
  11.4 9.4 %collective-permute-start.6 = (f32[128,256]{1,0:T(8,128)S(1)}, f32[128,256]{1,0:T(8,128)S(1)}, u32[]{:S(2)}, u32[]{:S(2)}) collective-permute-start(f32[128,256]{1,0:T(8,128)S(1)} %collective-permute-done.refs_4_), channel_id=1, source_target_pairs={{0,64},{64,128},{128,192},{192,0},{1,65},{65,129},{129,193},{193,1... | collective-permute-start | bytes 393224 | tf_op jit(solution)/shard_map/ppermute | solution.py:32
  14.7 9.9 %collective-permute-start.8 = (f32[256,256]{1,0:T(8,128)S(1)}, f32[256,256]{1,0:T(8,128)S(1)}, u32[]{:S(2)}, u32[]{:S(2)}) collective-permute-start(f32[256,256]{1,0:T(8,128)S(1)} %pad_maximum_fusion.4), channel_id=1, source_target_pairs={{0,16},{16,0},{1,17},{17,1},{2,18},{18,2},{3,19},{19,3},{4,20},{20... | collective-permute-start | bytes 786440 | tf_op jit(solution)/shard_map/ppermute | solution.py:32
  14.8 9.8 %collective-permute-start.7 = (f32[256,256]{1,0:T(8,128)S(1)}, f32[256,256]{1,0:T(8,128)S(1)}, u32[]{:S(2)}, u32[]{:S(2)}) collective-permute-start(f32[256,256]{1,0:T(8,128)S(1)} %pad_maximum_fusion.3), channel_id=1, source_target_pairs={{0,16},{16,0},{1,17},{17,1},{2,18},{18,2},{3,19},{19,3},{4,20},{20... | collective-permute-start | bytes 786440 | tf_op jit(solution)/shard_map/ppermute | solution.py:32
  17.3 6.8 %collective-permute-start.5 = (f32[128,256]{1,0:T(8,128)S(1)}, f32[128,256]{1,0:T(8,128)S(1)}, u32[]{:S(2)}, u32[]{:S(2)}) collective-permute-start(f32[128,256]{1,0:T(8,128)S(1)} %collective-permute-done.4.refs_9_), channel_id=1, source_target_pairs={{0,64},{64,128},{128,192},{192,0},{1,65},{65,129},{129,193},{193,1... | collective-permute-start | bytes 393224 | tf_op jit(solution)/shard_map/ppermute | solution.py:32
  17.4 6.6 %collective-permute-start.2 = (f32[128,256]{1,0:T(8,128)S(1)}, f32[128,256]{1,0:T(8,128)S(1)}, u32[]{:S(2)}, u32[]{:S(2)}) collective-permute-start(f32[128,256]{1,0:T(8,128)S(1)} %collective-permute-done.1.refs_6_), channel_id=1, source_target_pairs={{0,192},{64,0},{128,64},{192,128},{1,193},{65,1},{129,65},{193,129... | collective-permute-start | bytes 393224 | tf_op jit(solution)/shard_map/ppermute | solution.py:32
  28.2 9.4 %collective-permute-start.15 = (f32[136,256]{1,0:T(8,128)S(1)}, f32[136,256]{1,0:T(8,128)S(1)}, u32[]{:S(2)}, u32[]{:S(2)}) collective-permute-start(f32[136,256]{1,0:T(8,128)S(1)} %get-tuple-element.88), channel_id=1, source_target_pairs={{0,14},{2,0},{4,2},{6,4},{8,6},{10,8},{12,10},{14,12},{1,15},{3,1}... | collective-permute-start | bytes 417800 | tf_op jit(solution)/shard_map/ppermute | solution.py:32
  34.2 6.9 %collective-permute-start.11 = (f32[136,256]{1,0:T(8,128)S(1)}, f32[136,256]{1,0:T(8,128)S(1)}, u32[]{:S(2)}, u32[]{:S(2)}) collective-permute-start(f32[136,256]{1,0:T(8,128)S(1)} %get-tuple-element.89), channel_id=1, source_target_pairs={{0,2},{2,4},{4,6},{6,8},{8,10},{10,12},{12,14},{14,0},{1,3},{3,5},... | collective-permute-start | bytes 417800 | tf_op jit(solution)/shard_map/ppermute | solution.py:32
  41.1 7.9 %collective-permute-start.16 = (f32[272,256]{1,0:T(8,128)S(1)}, f32[272,256]{1,0:T(8,128)S(1)}, u32[]{:S(2)}, u32[]{:S(2)}) collective-permute-start(f32[272,256]{1,0:T(8,128)S(1)} %get-tuple-element.86), channel_id=1, source_target_pairs={{0,14},{2,0},{4,2},{6,4},{8,6},{10,8},{12,10},{14,12},{1,15},{3,1}... | collective-permute-start | bytes 835592 | tf_op jit(solution)/shard_map/ppermute | solution.py:32
  41.4 9.5 %collective-permute-start.12 = (f32[272,256]{1,0:T(8,128)S(1)}, f32[272,256]{1,0:T(8,128)S(1)}, u32[]{:S(2)}, u32[]{:S(2)}) collective-permute-start(f32[272,256]{1,0:T(8,128)S(1)} %get-tuple-element.87), channel_id=1, source_target_pairs={{0,2},{2,4},{4,6},{6,8},{8,10},{10,12},{12,14},{14,0},{1,3},{3,5},... | collective-permute-start | bytes 835592 | tf_op jit(solution)/shard_map/ppermute | solution.py:32
  49.0 7.0 %collective-permute-start.17 = (f32[272,256]{1,0:T(8,128)S(1)}, f32[272,256]{1,0:T(8,128)S(1)}, u32[]{:S(2)}, u32[]{:S(2)}) collective-permute-start(f32[272,256]{1,0:T(8,128)S(1)} %bitcast_add_fusion.1), channel_id=1, source_target_pairs={{0,14},{2,0},{4,2},{6,4},{8,6},{10,8},{12,10},{14,12},{1,15},{3,1}... | collective-permute-start | bytes 835592 | tf_op jit(solution)/shard_map/ppermute | solution.py:32
  50.9 8.5 %collective-permute-start.13 = (f32[272,256]{1,0:T(8,128)S(1)}, f32[272,256]{1,0:T(8,128)S(1)}, u32[]{:S(2)}, u32[]{:S(2)}) collective-permute-start(f32[272,256]{1,0:T(8,128)S(1)} %bitcast_add_fusion.3), channel_id=1, source_target_pairs={{0,2},{2,4},{4,6},{6,8},{8,10},{10,12},{12,14},{14,0},{1,3},{3,5},... | collective-permute-start | bytes 835592 | tf_op jit(solution)/shard_map/ppermute | solution.py:32
  56.0 7.5 %collective-permute-start.18 = (f32[272,256]{1,0:T(8,128)S(1)}, f32[272,256]{1,0:T(8,128)S(1)}, u32[]{:S(2)}, u32[]{:S(2)}) collective-permute-start(f32[272,256]{1,0:T(8,128)S(1)} %bitcast_add_fusion), channel_id=1, source_target_pairs={{0,14},{2,0},{4,2},{6,4},{8,6},{10,8},{12,10},{14,12},{1,15},{3,1}... | collective-permute-start | bytes 835592 | tf_op jit(solution)/shard_map/ppermute | solution.py:32
  59.5 7.8 %collective-permute-start.14 = (f32[272,256]{1,0:T(8,128)S(1)}, f32[272,256]{1,0:T(8,128)S(1)}, u32[]{:S(2)}, u32[]{:S(2)}) collective-permute-start(f32[272,256]{1,0:T(8,128)S(1)} %bitcast_add_fusion.2), channel_id=1, source_target_pairs={{0,2},{2,4},{4,6},{6,8},{8,10},{10,12},{12,14},{14,0},{1,3},{3,5},... | collective-permute-start | bytes 835592 | tf_op jit(solution)/shard_map/ppermute | solution.py:32
  80.1 15.3 %collective-permute-start.23 = (f32[256,256]{1,0:T(8,128)S(1)}, f32[256,256]{1,0:T(8,128)S(1)}, u32[]{:S(2)}, u32[]{:S(2)}) collective-permute-start(f32[256,256]{1,0:T(8,128)S(1)} %constant_dynamic-update-slice_fusion.refs_3_), channel_id=1, source_target_pairs={{0,14},{2,0},{4,2},{6,4},{8,6},{10,8},{12,10},{14,12},{1,15},{3,1}... | collective-permute-start | bytes 786440 | tf_op jit(solution)/shard_map/ppermute | solution.py:32
  80.2 15.2 %collective-permute-start.22 = (f32[256,256]{1,0:T(8,128)S(1)}, f32[256,256]{1,0:T(8,128)S(1)}, u32[]{:S(2)}, u32[]{:S(2)}) collective-permute-start(f32[256,256]{1,0:T(8,128)S(1)} %constant_dynamic-update-slice_fusion.refs_3_), channel_id=1, source_target_pairs={{0,2},{2,4},{4,6},{6,8},{8,10},{10,12},{12,14},{14,0},{1,3},{3,5},... | collective-permute-start | bytes 786440 | tf_op jit(solution)/shard_map/ppermute | solution.py:32
  95.5 7.9 %collective-permute-start.24 = (f32[280,256]{1,0:T(8,128)S(1)}, f32[280,256]{1,0:T(8,128)S(1)}, u32[]{:S(2)}, u32[]{:S(2)}) collective-permute-start(f32[280,256]{1,0:T(8,128)S(1)} %get-tuple-element.103), channel_id=1, source_target_pairs={{0,2},{2,4},{4,6},{6,8},{8,10},{10,12},{12,14},{14,0},{1,3},{3,5},... | collective-permute-start | bytes 860168 | tf_op jit(solution)/shard_map/ppermute | solution.py:32
  95.6 7.8 %collective-permute-start.25 = (f32[280,256]{1,0:T(8,128)S(1)}, f32[280,256]{1,0:T(8,128)S(1)}, u32[]{:S(2)}, u32[]{:S(2)}) collective-permute-start(f32[280,256]{1,0:T(8,128)S(1)} %get-tuple-element.102), channel_id=1, source_target_pairs={{0,14},{2,0},{4,2},{6,4},{8,6},{10,8},{12,10},{14,12},{1,15},{3,1}... | collective-permute-start | bytes 860168 | tf_op jit(solution)/shard_map/ppermute | solution.py:32
  103.4 8.4 %collective-permute-start.26 = (f32[280,256]{1,0:T(8,128)S(1)}, f32[280,256]{1,0:T(8,128)S(1)}, u32[]{:S(2)}, u32[]{:S(2)}) collective-permute-start(f32[280,256]{1,0:T(8,128)S(1)} %collective-permute-done.24.refs_6_), channel_id=1, source_target_pairs={{0,2},{2,4},{4,6},{6,8},{8,10},{10,12},{12,14},{14,0},{1,3},{3,5},... | collective-permute-start | bytes 860168 | tf_op jit(solution)/shard_map/ppermute | solution.py:32
  103.4 8.5 %collective-permute-start.27 = (f32[280,256]{1,0:T(8,128)S(1)}, f32[280,256]{1,0:T(8,128)S(1)}, u32[]{:S(2)}, u32[]{:S(2)}) collective-permute-start(f32[280,256]{1,0:T(8,128)S(1)} %collective-permute-done.25.refs_7_), channel_id=1, source_target_pairs={{0,14},{2,0},{4,2},{6,4},{8,6},{10,8},{12,10},{14,12},{1,15},{3,1}... | collective-permute-start | bytes 860168 | tf_op jit(solution)/shard_map/ppermute | solution.py:32
  111.9 6.6 %collective-permute-start.28 = (f32[152,256]{1,0:T(8,128)S(1)}, f32[152,256]{1,0:T(8,128)S(1)}, u32[]{:S(2)}, u32[]{:S(2)}) collective-permute-start(f32[152,256]{1,0:T(8,128)S(1)} %pad_maximum_fusion.8), channel_id=1, source_target_pairs={{0,2},{2,4},{4,6},{6,8},{8,10},{10,12},{12,14},{14,0},{1,3},{3,5},... | collective-permute-start | bytes 466952 | tf_op jit(solution)/shard_map/ppermute | solution.py:32
  112.0 6.5 %collective-permute-start.29 = (f32[152,256]{1,0:T(8,128)S(1)}, f32[152,256]{1,0:T(8,128)S(1)}, u32[]{:S(2)}, u32[]{:S(2)}) collective-permute-start(f32[152,256]{1,0:T(8,128)S(1)} %slice.223), channel_id=1, source_target_pairs={{0,14},{2,0},{4,2},{6,4},{8,6},{10,8},{12,10},{14,12},{1,15},{3,1}... | collective-permute-start | bytes 466952 | tf_op jit(solution)/shard_map/ppermute | solution.py:32
  (13 other events, 108.9 us)

commit v3 on v2

--- a/solution.py
+++ b/solution.py
@@ -19,8 +19,8 @@
 BLOCK = F + COUNT
 SHARE = 16
 PIECE = SHARE + 8
-CUTS = (0, 8, 16, TMAX)
-PARTS = len(CUTS) - 1
+PARTS = 8
+LISTED = TMAX // PARTS
 highest = lax.Precision.HIGHEST
 f32 = jnp.float32
 bf16 = jnp.bfloat16
@@ -60,46 +60,59 @@
     return ((z - lax.axis_index("z")) & 7) * 2 + (yl ^ lax.axis_index("yl"))
 
 
-def over_tiles(mask_refs, use):
-    for start, ref in zip(CUTS, mask_refs):
-        for k in range(ref.shape[0]):
-            use(start + k, ref[k].astype(f32).astype(bf16))
-
-
-def forward_body(index_ref, *refs):
-    masks, sources, (out_ref, held) = refs[:PARTS], refs[PARTS:-2], refs[-2:]
+def widen(mask):
+    return mask.astype(f32).astype(bf16)
+
+
+def forward_body(index_ref, mask_ref, *refs):
+    sources, (out_ref, narrow_ref, held, wide, arrived) = refs[:-5], refs[-5:]
+    copies = []
+    for part in range(PARTS):
+        rows = pl.ds(part * LISTED, LISTED)
+        copies.append(pltpu.make_async_copy(mask_ref.at[rows], wide.at[rows], arrived.at[part]))
+        copies[-1].start()
     for slot in range(BLOCKS):
         high, low = split_terms(sources[slot][...])
         held[slot, :F, :] = high
         held[slot, F : 2 * F, :] = low
         held[slot, 2 * F :, :] = jnp.ones((16, TILE), bf16)
     out_ref[...] = jnp.zeros_like(out_ref)
-
-    def use(tile, mask):
+    for tile in range(TMAX):
+        if tile % LISTED == 0:
+            copies[tile // LISTED].wait()
         target = target_slot(index_ref[0, tile])
         source = source_slot(index_ref[1, tile])
+        mask = wide[tile]
+        narrow_ref[tile] = mask.astype(jnp.int8)
         product = lax.dot_general(
-            held[source], mask, (((1,), (1,)), ((), ())), preferred_element_type=f32
+            held[source], widen(mask), (((1,), (1,)), ((), ())), preferred_element_type=f32
         )
         out_ref[target, :F, :] += product[:F] + product[F : 2 * F]
         out_ref[target, F:, :] += product[2 * F : 2 * F + COUNT]
 
-    over_tiles(masks, use)
-
 
 def vmem(count):
-    return [pl.BlockSpec(memory_space=pltpu.SMEM)] + [pl.BlockSpec(memory_space=pltpu.VMEM)] * count
-
-
-def forward_products(index, masks, sources):
+    return [pl.BlockSpec(memory_space=pltpu.VMEM)] * count
+
+
+def forward_products(index, mask, sources):
     return pl.pallas_call(
         forward_body,
-        in_specs=vmem(PARTS + BLOCKS),
-        out_shape=jax.ShapeDtypeStruct((BLOCKS, BLOCK, TILE), f32),
-        scratch_shapes=[pltpu.VMEM((BLOCKS, 2 * F + 16, TILE), bf16)],
-        compiler_params=params(24),
+        in_specs=[pl.BlockSpec(memory_space=pltpu.SMEM), pl.BlockSpec(memory_space=pl.ANY)]
+        + vmem(BLOCKS),
+        out_specs=tuple(vmem(2)),
+        out_shape=(
+            jax.ShapeDtypeStruct((BLOCKS, BLOCK, TILE), f32),
+            jax.ShapeDtypeStruct((TMAX, TILE, TILE), jnp.int8),
+        ),
+        scratch_shapes=[
+            pltpu.VMEM((BLOCKS, 2 * F + 16, TILE), bf16),
+            pltpu.VMEM((TMAX, TILE, TILE), jnp.int32),
+            pltpu.SemaphoreType.DMA((PARTS,)),
+        ],
+        compiler_params=params(46),
         cost_estimate=cost(TMAX),
-    )(index, *masks, *sources)
+    )(index, mask, *sources)
 
 
 def dense_body(a_ref, b_ref, c_ref, d_ref, x_ref, w_ref, o_ref, g_ref, hidden_ref, out_ref, gw_ref):
@@ -136,8 +149,8 @@
     )(*parts, x_t, weight, offset.reshape(1, H), cotangent)
 
 
-def backward_body(index_ref, *refs):
-    masks, ins, (near_ref, far_ref, held, sums) = refs[:PARTS], refs[PARTS:-4], refs[-4:]
+def backward_body(index_ref, mask_ref, *refs):
+    ins, (near_ref, far_ref, held, sums) = refs[:-4], refs[-4:]
     places = [(0, 0), (7, 1), (1, 2), (6, 3), (2, 4), (5, 5), (3, 6)]
     parts = [(2 * z + h, ins[k], h * F) for z, k in places for h in range(2)]
     parts += [(8, ins[7], 0), (9, ins[8], 0)]
@@ -147,23 +160,20 @@
         held[slot, F:, :] = low
     sums[...] = jnp.zeros_like(sums)
     core = lax.axis_index("core")
-
-    def use(tile, mask):
+    for tile in range(TMAX):
         source = target_slot(index_ref[0, tile])
         block = index_ref[1, tile]
-        product = jnp.dot(held[source], mask, preferred_element_type=f32)
+        product = jnp.dot(held[source], widen(mask_ref[tile]), preferred_element_type=f32)
         sums[((block & 1) ^ core) * 8 + (block >> 1)] += product[:F] + product[F:]
-
-    over_tiles(masks, use)
     near_ref[...] = sums[:8]
     far_ref[...] = sums[8:]
 
 
-def backward_products(index, masks, gathered):
+def backward_products(index, mask, gathered):
     half = jax.ShapeDtypeStruct((8, F, TILE), f32)
     return pl.pallas_call(
         backward_body,
-        in_specs=vmem(PARTS + len(gathered)),
+        in_specs=[pl.BlockSpec(memory_space=pltpu.SMEM)] + vmem(1 + len(gathered)),
         out_shape=(half, half),
         scratch_shapes=[
             pltpu.VMEM((BLOCKS, 2 * F, TILE), bf16),
@@ -171,7 +181,7 @@
         ],
         compiler_params=params(24),
         cost_estimate=cost(TMAX),
-    )(index, *masks, *gathered)
+    )(index, mask, *gathered)
 
 
 SCALE = 1.0 / float(np.sqrt(BLOCKS * BLOCKS * TILE))
@@ -198,17 +208,11 @@
     )(parts, outgoing, piece)
 
 
-def gather_row(x_t, mask):
+def gather_row(x_t):
     h = shift(x_t, "yh", 1)
     r1, l1 = shift(x_t, "x", 1), shift(x_t, "x", -1)
-    narrow = lambda whole, k: whole[CUTS[k] : CUTS[k + 1]].astype(jnp.int8)
-    m0 = narrow(mask, 0)
-    h, m0, mask = together((h, m0, mask))
     r1h, l1h = shift(h, "x", 1), shift(h, "x", -1)
-    m1 = narrow(mask, 1)
-    l1h, m1, mask = together((l1h, m1, mask))
     r2, l2 = shift(r1, "x", 1), shift(l1h, "x", -1)
-    l2, m2 = together((l2, narrow(mask, 2)))
     own = [x_t, h, l1, l1h, r2, l2, r1, r1h]
     pairs = [[x_t, h], [l1, r1], [l1h, r1h], [r2, l2]]
     far = []
@@ -216,7 +220,7 @@
         both = shift(jnp.concatenate([a, b], axis=0), "core", 1)
         far.append((both[:F], both[F:]))
     (f0, f1), (f2, f6), (f3, f7), (f4, f5) = far
-    return own + [f0, f1, f2, f3, f4, f5, f6, f7], (m0, m1, m2)
+    return own + [f0, f1, f2, f3, f4, f5, f6, f7]
 
 
 def scatter_col(sums):
@@ -255,8 +259,8 @@
     return (both, r1, l1, r2, l2, r3, l3, r4, l4), piece, r4[F:]
 
 
-def scatter_row(index, masks, gathered, piece, last):
-    (near, far), last = together((backward_products(index, masks, gathered), shift(last, "z", 1)))
+def scatter_row(index, mask, gathered, piece, last):
+    (near, far), last = together((backward_products(index, mask, gathered), shift(last, "z", 1)))
     piece = piece + last
     got, piece = together((shift(far, "core", 1), piece + shift(piece, "yl", 1)))
     share = jnp.broadcast_to(piece[:SHARE], (8, SHARE, H))
@@ -267,11 +271,12 @@
 def per_device(features, weight, offset, cotangent, tile_index, edge_mask):
     index = tile_index.reshape(2, TMAX)
     x_t = features.T
-    sources, masks = gather_row(x_t, edge_mask.reshape(TMAX, TILE, TILE))
-    parts = scatter_col(forward_products(index, masks, sources))
+    mask = edge_mask.reshape(TMAX, TILE, TILE)
+    sums, mask = forward_products(index, mask, gather_row(x_t))
+    parts = scatter_col(sums)
     hidden, outgoing, gw = dense(parts, x_t, weight, offset, cotangent)
     gathered, piece, last = gather_col(outgoing, gw)
-    parts, piece = scatter_row(index, masks, gathered, piece, last)
+    parts, piece = scatter_row(index, mask, gathered, piece, last)
     grad, grad_weight, grad_offset = finish(parts, outgoing, piece)
     return hidden, grad, grad_weight, grad_offset.reshape(H)
 

time: 149 us -> 149 us (level)
  other arithmetic: 7.4 us -> 0.71 us
  Pallas kernels: 7.17 us -> 9.49 us
  waiting for transfers between devices: 56.6 us -> 58.4 us
    another operation x2 -> x0, other arithmetic: 4.92 us -> none
    pallas_call x2, Pallas kernels: 4.72 us -> 7.06 us  [the longest x1 4.74 us: forward_products(): pl.pallas_call(forward_body, in_specs=[pl.BlockSpec(memory_space=pltpu.SM...]
    ppermute x33, waiting for transfers between devices: 56.6 us -> 58.4 us  [shift(): lax.ppermute(value, axis, [(i, (i + by) % size) for i in range(size)])]
    convert_element_type x1 -> x0, other arithmetic: 1.76 us -> none  [gather_row(): narrow = lambda whole, k: whole[CUTS[k]:CUTS[k + 1]].astype(jnp.int8)]
  transfers between devices with their start and end apart: 33 -> 33, of which waited for: 17 -> 19; matrix products, arithmetic and copies ran while one was open for 5% -> 0% of each run, Pallas kernels for 2% -> 2%
where the time goes in v3:
time: 149 us; the launch traced here: 148 us
  waiting for transfers between devices  58.4 us (39%)
  starting transfers between devices  42.3 us (28%)
  blocking collectives  35.1 us (24%)
  Pallas kernels  9.49 us (6%)
    ppermute x33, waiting for transfers between devices, shift(): lax.ppermute(value, axis, [(i, (i + by) % size) for i in range(size)])  58.4 us
    ppermute x33, starting transfers between devices, shift(): lax.ppermute(value, axis, [(i, (i + by) % size) for i in range(size)])  42.3 us
    all_to_all x1, blocking collectives, scatter_row(): return (lax.all_to_all(total, PLANE, 0, 0, tiled=True), piece)  20.7 us
    all_to_all x1, blocking collectives, gather_col(): lax.all_to_all(shares, PLANE, 0, 0, tiled=True)  14.4 us
    pallas_call x1, Pallas kernels, forward_products(): pl.pallas_call(forward_body, in_specs=[pl.BlockSpec(memory_space=pltpu.SM...  4.74 us
  transfers between devices with their start and end apart: 33, of which 19 were waited for; matrix products, arithmetic and copies ran while one was open for 0% of the time, Pallas kernels for 2%

profile of v3, /device:TPU:8, one launch (start us, length us, event | category | flops | bytes accessed | tf_op | source)
XLA Modules:
  0.0 148.4 jit_solution(14145030928358405210)
XLA Ops:
  1.7 2.4 %collective-permute-start = (f32[128,256]{1,0:T(8,128)S(1)}, f32[128,256]{1,0:T(8,128)S(1)}, u32[]{:S(2)}, u32[]{:S(2)}) collective-permute-start(f32[128,256]{1,0:T(8,128)S(1)} %bitcast.32), channel_id=1, source_target_pairs={{0,32},{32,0},{1,33},{33,1},{2,34},{34,2},{3,35},{35,3},{4,36},{36... | collective-permute-start | bytes 393224 | tf_op jit(solution)/shard_map/ppermute | solution.py:32
  8.5 2.8 %collective-permute-start.2 = (f32[128,256]{1,0:T(8,128)S(1)}, f32[128,256]{1,0:T(8,128)S(1)}, u32[]{:S(2)}, u32[]{:S(2)}) collective-permute-start(f32[128,256]{1,0:T(8,128)S(1)} %collective-permute-done.refs_1_), channel_id=1, source_target_pairs={{0,192},{64,0},{128,64},{192,128},{1,193},{65,1},{129,65},{193,129... | collective-permute-start | bytes 393224 | tf_op jit(solution)/shard_map/ppermute | solution.py:32
  13.8 3.7 %collective-permute-start.5 = (f32[128,256]{1,0:T(8,128)S(1)}, f32[128,256]{1,0:T(8,128)S(1)}, u32[]{:S(2)}, u32[]{:S(2)}) collective-permute-start(f32[128,256]{1,0:T(8,128)S(1)} %collective-permute-done.2.refs_3_), channel_id=1, source_target_pairs={{0,192},{64,0},{128,64},{192,128},{1,193},{65,1},{129,65},{193,129... | collective-permute-start | bytes 393224 | tf_op jit(solution)/shard_map/ppermute | solution.py:32
  21.8 4.7 %shard_map.93 = (f32[16,136,256]{2,1,0:T(8,128)S(1)}, s8[32,256,256]{2,1,0:T(32,128)(4,1)S(1)}) custom-call(s32[2,32]{1,0:T(2,128)S(1)} %bitcast.38, s32[32,256,256]{2,1,0:T(8,128)} %bitcast.41, f32[128,256]{1,0:T(8,128)S(1)} %bitcast.36, f32[128,256]{1,0:T(8,128)S(1)} %collective-permute-done.refs_1_, f32[128,256]{1,0:T(8,128)S(1)} %collective-permute-done.1.refs_2_, ...), custom_call_target="tpu_custom_call" | custom-call | flops 1073741824 | bytes 4194304 | tf_op jit(solution)/shard_map/pallas_call | solution.py:99
  26.6 5.9 %collective-permute-start.15 = (f32[136,256]{1,0:T(8,128)S(1)}, f32[136,256]{1,0:T(8,128)S(1)}, u32[]{:S(2)}, u32[]{:S(2)}) collective-permute-start(f32[136,256]{1,0:T(8,128)S(1)} %get-tuple-element.76), channel_id=1, source_target_pairs={{0,14},{2,0},{4,2},{6,4},{8,6},{10,8},{12,10},{14,12},{1,15},{3,1}... | collective-permute-start | bytes 417800 | tf_op jit(solution)/shard_map/ppermute | solution.py:32
  32.7 3.1 %collective-permute-done.15 = f32[136,256]{1,0:T(8,128)S(1)} collective-permute-done((f32[136,256]{1,0:T(8,128)S(1)}, f32[136,256]{1,0:T(8,128)S(1)}, u32[]{:S(2)}, u32[]{:S(2)}) %collective-permute-start.15) | collective-permute-done | bytes 139296 | tf_op jit(solution)/shard_map/ppermute | solution.py:32
  35.8 3.4 %collective-permute-done.11 = f32[136,256]{1,0:T(8,128)S(1)} collective-permute-done((f32[136,256]{1,0:T(8,128)S(1)}, f32[136,256]{1,0:T(8,128)S(1)}, u32[]{:S(2)}, u32[]{:S(2)}) %collective-permute-start.11) | collective-permute-done | bytes 139296 | tf_op jit(solution)/shard_map/ppermute | solution.py:32
  41.5 5.5 %collective-permute-done.16 = f32[272,256]{1,0:T(8,128)S(1)} collective-permute-done((f32[272,256]{1,0:T(8,128)S(1)}, f32[272,256]{1,0:T(8,128)S(1)}, u32[]{:S(2)}, u32[]{:S(2)}) %collective-permute-start.16) | collective-permute-done | bytes 278560 | tf_op jit(solution)/shard_map/ppermute | solution.py:32
  49.3 4.6 %collective-permute-done.17 = f32[272,256]{1,0:T(8,128)S(1)} collective-permute-done((f32[272,256]{1,0:T(8,128)S(1)}, f32[272,256]{1,0:T(8,128)S(1)}, u32[]{:S(2)}, u32[]{:S(2)}) %collective-permute-start.17) | collective-permute-done | bytes 278560 | tf_op jit(solution)/shard_map/ppermute | solution.py:32
  53.9 3.3 %collective-permute-start.18 = (f32[272,256]{1,0:T(8,128)S(1)}, f32[272,256]{1,0:T(8,128)S(1)}, u32[]{:S(2)}, u32[]{:S(2)}) collective-permute-start(f32[272,256]{1,0:T(8,128)S(1)} %bitcast_add_fusion), channel_id=1, source_target_pairs={{0,14},{2,0},{4,2},{6,4},{8,6},{10,8},{12,10},{14,12},{1,15},{3,1}... | collective-permute-start | bytes 835592 | tf_op jit(solution)/shard_map/ppermute | solution.py:32
  57.4 3.9 %collective-permute-done.18 = f32[272,256]{1,0:T(8,128)S(1)} collective-permute-done((f32[272,256]{1,0:T(8,128)S(1)}, f32[272,256]{1,0:T(8,128)S(1)}, u32[]{:S(2)}, u32[]{:S(2)}) %collective-permute-start.18) | collective-permute-done | bytes 278560 | tf_op jit(solution)/shard_map/ppermute | solution.py:32
  61.4 3.8 %collective-permute-done.14 = f32[272,256]{1,0:T(8,128)S(1)} collective-permute-done((f32[272,256]{1,0:T(8,128)S(1)}, f32[272,256]{1,0:T(8,128)S(1)}, u32[]{:S(2)}, u32[]{:S(2)}) %collective-permute-start.14) | collective-permute-done | bytes 278560 | tf_op jit(solution)/shard_map/ppermute | solution.py:32
  65.9 4.5 %collective-permute-done.19.d_ref = f32[136,256]{1,0:T(8,128)S(1)} collective-permute-done((f32[136,256]{1,0:T(8,128)S(1)}, f32[136,256]{1,0:T(8,128)S(1)}, u32[]{:S(2)}, u32[]{:S(2)}) %collective-permute-start.19) | collective-permute-done | bytes 139296 | tf_op jit(solution)/shard_map/ppermute | solution.py:32
  73.4 4.5 %collective-permute-done.20 = f32[128,256]{1,0:T(8,128)S(1)} collective-permute-done((f32[128,256]{1,0:T(8,128)S(1)}, f32[128,256]{1,0:T(8,128)S(1)}, u32[]{:S(2)}, u32[]{:S(2)}) %collective-permute-start.20) | collective-permute-done | bytes 131104 | tf_op jit(solution)/shard_map/ppermute | solution.py:32
  80.1 14.4 %all_to_all.10 = f32[8,24,256]{2,1,0:T(8,128)S(1)} all-to-all(f32[8,24,256]{2,1,0:T(8,128)S(1)} %pad_maximum_fusion.7), channel_id=1, replica_groups=mesh['x'=4,'yh'=2,'core'=2,'z'=8,'yl'=2] {'x','yh'}, dimensions={0} | all-to-all | bytes 393216 | tf_op jit(solution)/shard_map/all_to_all | solution.py:248
  94.7 3.2 %collective-permute-start.25 = (f32[280,256]{1,0:T(8,128)S(1)}, f32[280,256]{1,0:T(8,128)S(1)}, u32[]{:S(2)}, u32[]{:S(2)}) collective-permute-start(f32[280,256]{1,0:T(8,128)S(1)} %get-tuple-element.90), channel_id=1, source_target_pairs={{0,14},{2,0},{4,2},{6,4},{8,6},{10,8},{12,10},{14,12},{1,15},{3,1}... | collective-permute-start | bytes 860168 | tf_op jit(solution)/shard_map/ppermute | solution.py:32
  97.9 4.6 %collective-permute-done.24.refs_3_ = f32[280,256]{1,0:T(8,128)S(1)} collective-permute-done((f32[280,256]{1,0:T(8,128)S(1)}, f32[280,256]{1,0:T(8,128)S(1)}, u32[]{:S(2)}, u32[]{:S(2)}) %collective-permute-start.24) | collective-permute-done | bytes 286752 | tf_op jit(solution)/shard_map/ppermute | solution.py:32
  102.6 3.2 %collective-permute-start.27 = (f32[280,256]{1,0:T(8,128)S(1)}, f32[280,256]{1,0:T(8,128)S(1)}, u32[]{:S(2)}, u32[]{:S(2)}) collective-permute-start(f32[280,256]{1,0:T(8,128)S(1)} %collective-permute-done.25.refs_4_), channel_id=1, source_target_pairs={{0,14},{2,0},{4,2},{6,4},{8,6},{10,8},{12,10},{14,12},{1,15},{3,1}... | collective-permute-start | bytes 860168 | tf_op jit(solution)/shard_map/ppermute | solution.py:32
  105.8 5.0 %collective-permute-done.26.refs_5_ = f32[280,256]{1,0:T(8,128)S(1)} collective-permute-done((f32[280,256]{1,0:T(8,128)S(1)}, f32[280,256]{1,0:T(8,128)S(1)}, u32[]{:S(2)}, u32[]{:S(2)}) %collective-permute-start.26) | collective-permute-done | bytes 286752 | tf_op jit(solution)/shard_map/ppermute | solution.py:32
  111.1 3.3 %collective-permute-start.29 = (f32[152,256]{1,0:T(8,128)S(1)}, f32[152,256]{1,0:T(8,128)S(1)}, u32[]{:S(2)}, u32[]{:S(2)}) collective-permute-start(f32[152,256]{1,0:T(8,128)S(1)} %slice.192), channel_id=1, source_target_pairs={{0,14},{2,0},{4,2},{6,4},{8,6},{10,8},{12,10},{14,12},{1,15},{3,1}... | collective-permute-start | bytes 466952 | tf_op jit(solution)/shard_map/ppermute | solution.py:32
  114.4 3.2 %collective-permute-done.28.refs_7_ = f32[152,256]{1,0:T(8,128)S(1)} collective-permute-done((f32[152,256]{1,0:T(8,128)S(1)}, f32[152,256]{1,0:T(8,128)S(1)}, u32[]{:S(2)}, u32[]{:S(2)}) %collective-permute-start.28) | collective-permute-done | bytes 155680 | tf_op jit(solution)/shard_map/ppermute | solution.py:32
  120.0 2.7 %collective-permute-done.30 = f32[24,256]{1,0:T(8,128)S(1)} collective-permute-done((f32[24,256]{1,0:T(8,128)S(1)}, f32[24,256]{1,0:T(8,128)S(1)}, u32[]{:S(2)}, u32[]{:S(2)}) %collective-permute-start.30) | collective-permute-done | bytes 24608 | tf_op jit(solution)/shard_map/ppermute | solution.py:32
  124.1 2.5 %collective-permute-done.32 = f32[24,256]{1,0:T(8,128)S(1)} collective-permute-done((f32[24,256]{1,0:T(8,128)S(1)}, f32[24,256]{1,0:T(8,128)S(1)}, u32[]{:S(2)}, u32[]{:S(2)}) %collective-permute-start.32) | collective-permute-done | bytes 24608 | tf_op jit(solution)/shard_map/ppermute | solution.py:32
  126.9 20.7 %all_to_all.11.parts_ref = f32[8,144,256]{2,1,0:T(8,128)S(1)} all-to-all(f32[8,144,256]{2,1,0:T(8,128)S(1)} %pad_maximum_fusion), channel_id=1, replica_groups=mesh['x'=4,'yh'=2,'core'=2,'z'=8,'yl'=2] {'x','yh'}, dimensions={0} | all-to-all | bytes 2359296 | tf_op jit(solution)/shard_map/all_to_all | solution.py:268
  (93 shorter events, 28.4 us)
Async XLA Ops:
  1.7 6.8 %collective-permute-start = (f32[128,256]{1,0:T(8,128)S(1)}, f32[128,256]{1,0:T(8,128)S(1)}, u32[]{:S(2)}, u32[]{:S(2)}) collective-permute-start(f32[128,256]{1,0:T(8,128)S(1)} %bitcast.32), channel_id=1, source_target_pairs={{0,32},{32,0},{1,33},{33,1},{2,34},{34,2},{3,35},{35,3},{4,36},{36... | collective-permute-start | bytes 393224 | tf_op jit(solution)/shard_map/ppermute | solution.py:32
  4.0 7.2 %collective-permute-start.3 = (f32[128,256]{1,0:T(8,128)S(1)}, f32[128,256]{1,0:T(8,128)S(1)}, u32[]{:S(2)}, u32[]{:S(2)}) collective-permute-start(f32[128,256]{1,0:T(8,128)S(1)} %bitcast.33), channel_id=1, source_target_pairs={{0,64},{64,128},{128,192},{192,0},{1,65},{65,129},{129,193},{193,1... | collective-permute-start | bytes 393224 | tf_op jit(solution)/shard_map/ppermute | solution.py:32
  5.5 5.7 %collective-permute-start.1 = (f32[128,256]{1,0:T(8,128)S(1)}, f32[128,256]{1,0:T(8,128)S(1)}, u32[]{:S(2)}, u32[]{:S(2)}) collective-permute-start(f32[128,256]{1,0:T(8,128)S(1)} %bitcast.34), channel_id=1, source_target_pairs={{0,192},{64,0},{128,64},{192,128},{1,193},{65,1},{129,65},{193,129... | collective-permute-start | bytes 393224 | tf_op jit(solution)/shard_map/ppermute | solution.py:32
  11.2 7.5 %collective-permute-start.6 = (f32[128,256]{1,0:T(8,128)S(1)}, f32[128,256]{1,0:T(8,128)S(1)}, u32[]{:S(2)}, u32[]{:S(2)}) collective-permute-start(f32[128,256]{1,0:T(8,128)S(1)} %collective-permute-done.refs_1_), channel_id=1, source_target_pairs={{0,64},{64,128},{128,192},{192,0},{1,65},{65,129},{129,193},{193,1... | collective-permute-start | bytes 393224 | tf_op jit(solution)/shard_map/ppermute | solution.py:32
  11.3 9.0 %collective-permute-start.8 = (f32[256,256]{1,0:T(8,128)S(1)}, f32[256,256]{1,0:T(8,128)S(1)}, u32[]{:S(2)}, u32[]{:S(2)}) collective-permute-start(f32[256,256]{1,0:T(8,128)S(1)} %pad_maximum_fusion.4), channel_id=1, source_target_pairs={{0,16},{16,0},{1,17},{17,1},{2,18},{18,2},{3,19},{19,3},{4,20},{20... | collective-permute-start | bytes 786440 | tf_op jit(solution)/shard_map/ppermute | solution.py:32
  11.4 8.8 %collective-permute-start.4 = (f32[128,256]{1,0:T(8,128)S(1)}, f32[128,256]{1,0:T(8,128)S(1)}, u32[]{:S(2)}, u32[]{:S(2)}) collective-permute-start(f32[128,256]{1,0:T(8,128)S(1)} %collective-permute-done.3.refs_6_), channel_id=1, source_target_pairs={{0,64},{64,128},{128,192},{192,0},{1,65},{65,129},{129,193},{193,1... | collective-permute-start | bytes 393224 | tf_op jit(solution)/shard_map/ppermute | solution.py:32
  13.8 6.4 %collective-permute-start.5 = (f32[128,256]{1,0:T(8,128)S(1)}, f32[128,256]{1,0:T(8,128)S(1)}, u32[]{:S(2)}, u32[]{:S(2)}) collective-permute-start(f32[128,256]{1,0:T(8,128)S(1)} %collective-permute-done.2.refs_3_), channel_id=1, source_target_pairs={{0,192},{64,0},{128,64},{192,128},{1,193},{65,1},{129,65},{193,129... | collective-permute-start | bytes 393224 | tf_op jit(solution)/shard_map/ppermute | solution.py:32
  26.6 9.1 %collective-permute-start.15 = (f32[136,256]{1,0:T(8,128)S(1)}, f32[136,256]{1,0:T(8,128)S(1)}, u32[]{:S(2)}, u32[]{:S(2)}) collective-permute-start(f32[136,256]{1,0:T(8,128)S(1)} %get-tuple-element.76), channel_id=1, source_target_pairs={{0,14},{2,0},{4,2},{6,4},{8,6},{10,8},{12,10},{14,12},{1,15},{3,1}... | collective-permute-start | bytes 417800 | tf_op jit(solution)/shard_map/ppermute | solution.py:32
  32.5 6.6 %collective-permute-start.11 = (f32[136,256]{1,0:T(8,128)S(1)}, f32[136,256]{1,0:T(8,128)S(1)}, u32[]{:S(2)}, u32[]{:S(2)}) collective-permute-start(f32[136,256]{1,0:T(8,128)S(1)} %get-tuple-element.77), channel_id=1, source_target_pairs={{0,2},{2,4},{4,6},{6,8},{8,10},{10,12},{12,14},{14,0},{1,3},{3,5},... | collective-permute-start | bytes 417800 | tf_op jit(solution)/shard_map/ppermute | solution.py:32
  39.3 7.8 %collective-permute-start.16 = (f32[272,256]{1,0:T(8,128)S(1)}, f32[272,256]{1,0:T(8,128)S(1)}, u32[]{:S(2)}, u32[]{:S(2)}) collective-permute-start(f32[272,256]{1,0:T(8,128)S(1)} %get-tuple-element.74), channel_id=1, source_target_pairs={{0,14},{2,0},{4,2},{6,4},{8,6},{10,8},{12,10},{14,12},{1,15},{3,1}... | collective-permute-start | bytes 835592 | tf_op jit(solution)/shard_map/ppermute | solution.py:32
  39.8 9.2 %collective-permute-start.12 = (f32[272,256]{1,0:T(8,128)S(1)}, f32[272,256]{1,0:T(8,128)S(1)}, u32[]{:S(2)}, u32[]{:S(2)}) collective-permute-start(f32[272,256]{1,0:T(8,128)S(1)} %get-tuple-element.75), channel_id=1, source_target_pairs={{0,2},{2,4},{4,6},{6,8},{8,10},{10,12},{12,14},{14,0},{1,3},{3,5},... | collective-permute-start | bytes 835592 | tf_op jit(solution)/shard_map/ppermute | solution.py:32
  47.1 6.8 %collective-permute-start.17 = (f32[272,256]{1,0:T(8,128)S(1)}, f32[272,256]{1,0:T(8,128)S(1)}, u32[]{:S(2)}, u32[]{:S(2)}) collective-permute-start(f32[272,256]{1,0:T(8,128)S(1)} %bitcast_add_fusion.1), channel_id=1, source_target_pairs={{0,14},{2,0},{4,2},{6,4},{8,6},{10,8},{12,10},{14,12},{1,15},{3,1}... | collective-permute-start | bytes 835592 | tf_op jit(solution)/shard_map/ppermute | solution.py:32
  49.1 8.2 %collective-permute-start.13 = (f32[272,256]{1,0:T(8,128)S(1)}, f32[272,256]{1,0:T(8,128)S(1)}, u32[]{:S(2)}, u32[]{:S(2)}) collective-permute-start(f32[272,256]{1,0:T(8,128)S(1)} %bitcast_add_fusion.3), channel_id=1, source_target_pairs={{0,2},{2,4},{4,6},{6,8},{8,10},{10,12},{12,14},{14,0},{1,3},{3,5},... | collective-permute-start | bytes 835592 | tf_op jit(solution)/shard_map/ppermute | solution.py:32
  53.9 7.4 %collective-permute-start.18 = (f32[272,256]{1,0:T(8,128)S(1)}, f32[272,256]{1,0:T(8,128)S(1)}, u32[]{:S(2)}, u32[]{:S(2)}) collective-permute-start(f32[272,256]{1,0:T(8,128)S(1)} %bitcast_add_fusion), channel_id=1, source_target_pairs={{0,14},{2,0},{4,2},{6,4},{8,6},{10,8},{12,10},{14,12},{1,15},{3,1}... | collective-permute-start | bytes 835592 | tf_op jit(solution)/shard_map/ppermute | solution.py:32
  57.3 7.8 %collective-permute-start.14 = (f32[272,256]{1,0:T(8,128)S(1)}, f32[272,256]{1,0:T(8,128)S(1)}, u32[]{:S(2)}, u32[]{:S(2)}) collective-permute-start(f32[272,256]{1,0:T(8,128)S(1)} %bitcast_add_fusion.2), channel_id=1, source_target_pairs={{0,2},{2,4},{4,6},{6,8},{8,10},{10,12},{12,14},{14,0},{1,3},{3,5},... | collective-permute-start | bytes 835592 | tf_op jit(solution)/shard_map/ppermute | solution.py:32
  72.0 5.9 %collective-permute-start.20 = (f32[128,256]{1,0:T(8,128)S(1)}, f32[128,256]{1,0:T(8,128)S(1)}, u32[]{:S(2)}, u32[]{:S(2)}) collective-permute-start(f32[128,256]{1,0:T(8,128)S(1)} %get-tuple-element.51.out_ref), channel_id=1, source_target_pairs={{0,1},{1,0},{2,3},{3,2},{4,5},{5,4},{6,7},{7,6},{8,9},{9,8},{10,11... | collective-permute-start | bytes 393224 | tf_op jit(solution)/shard_map/ppermute | solution.py:32
  78.0 16.6 %collective-permute-start.23 = (f32[256,256]{1,0:T(8,128)S(1)}, f32[256,256]{1,0:T(8,128)S(1)}, u32[]{:S(2)}, u32[]{:S(2)}) collective-permute-start(f32[256,256]{1,0:T(8,128)S(1)} %constant_dynamic-update-slice_fusion.refs_0_), channel_id=1, source_target_pairs={{0,14},{2,0},{4,2},{6,4},{8,6},{10,8},{12,10},{14,12},{1,15},{3,1}... | collective-permute-start | bytes 786440 | tf_op jit(solution)/shard_map/ppermute | solution.py:32
  78.1 16.5 %collective-permute-start.22 = (f32[256,256]{1,0:T(8,128)S(1)}, f32[256,256]{1,0:T(8,128)S(1)}, u32[]{:S(2)}, u32[]{:S(2)}) collective-permute-start(f32[256,256]{1,0:T(8,128)S(1)} %constant_dynamic-update-slice_fusion.refs_0_), channel_id=1, source_target_pairs={{0,2},{2,4},{4,6},{6,8},{8,10},{10,12},{12,14},{14,0},{1,3},{3,5},... | collective-permute-start | bytes 786440 | tf_op jit(solution)/shard_map/ppermute | solution.py:32
  94.6 7.9 %collective-permute-start.24 = (f32[280,256]{1,0:T(8,128)S(1)}, f32[280,256]{1,0:T(8,128)S(1)}, u32[]{:S(2)}, u32[]{:S(2)}) collective-permute-start(f32[280,256]{1,0:T(8,128)S(1)} %get-tuple-element.91), channel_id=1, source_target_pairs={{0,2},{2,4},{4,6},{6,8},{8,10},{10,12},{12,14},{14,0},{1,3},{3,5},... | collective-permute-start | bytes 860168 | tf_op jit(solution)/shard_map/ppermute | solution.py:32
  94.7 7.8 %collective-permute-start.25 = (f32[280,256]{1,0:T(8,128)S(1)}, f32[280,256]{1,0:T(8,128)S(1)}, u32[]{:S(2)}, u32[]{:S(2)}) collective-permute-start(f32[280,256]{1,0:T(8,128)S(1)} %get-tuple-element.90), channel_id=1, source_target_pairs={{0,14},{2,0},{4,2},{6,4},{8,6},{10,8},{12,10},{14,12},{1,15},{3,1}... | collective-permute-start | bytes 860168 | tf_op jit(solution)/shard_map/ppermute | solution.py:32
  102.5 8.2 %collective-permute-start.26 = (f32[280,256]{1,0:T(8,128)S(1)}, f32[280,256]{1,0:T(8,128)S(1)}, u32[]{:S(2)}, u32[]{:S(2)}) collective-permute-start(f32[280,256]{1,0:T(8,128)S(1)} %collective-permute-done.24.refs_3_), channel_id=1, source_target_pairs={{0,2},{2,4},{4,6},{6,8},{8,10},{10,12},{12,14},{14,0},{1,3},{3,5},... | collective-permute-start | bytes 860168 | tf_op jit(solution)/shard_map/ppermute | solution.py:32
  102.6 8.5 %collective-permute-start.27 = (f32[280,256]{1,0:T(8,128)S(1)}, f32[280,256]{1,0:T(8,128)S(1)}, u32[]{:S(2)}, u32[]{:S(2)}) collective-permute-start(f32[280,256]{1,0:T(8,128)S(1)} %collective-permute-done.25.refs_4_), channel_id=1, source_target_pairs={{0,14},{2,0},{4,2},{6,4},{8,6},{10,8},{12,10},{14,12},{1,15},{3,1}... | collective-permute-start | bytes 860168 | tf_op jit(solution)/shard_map/ppermute | solution.py:32
  110.8 6.8 %collective-permute-start.28 = (f32[152,256]{1,0:T(8,128)S(1)}, f32[152,256]{1,0:T(8,128)S(1)}, u32[]{:S(2)}, u32[]{:S(2)}) collective-permute-start(f32[152,256]{1,0:T(8,128)S(1)} %pad_maximum_fusion.8), channel_id=1, source_target_pairs={{0,2},{2,4},{4,6},{6,8},{8,10},{10,12},{12,14},{14,0},{1,3},{3,5},... | collective-permute-start | bytes 466952 | tf_op jit(solution)/shard_map/ppermute | solution.py:32
  111.1 6.5 %collective-permute-start.29 = (f32[152,256]{1,0:T(8,128)S(1)}, f32[152,256]{1,0:T(8,128)S(1)}, u32[]{:S(2)}, u32[]{:S(2)}) collective-permute-start(f32[152,256]{1,0:T(8,128)S(1)} %slice.192), channel_id=1, source_target_pairs={{0,14},{2,0},{4,2},{6,4},{8,6},{10,8},{12,10},{14,12},{1,15},{3,1}... | collective-permute-start | bytes 466952 | tf_op jit(solution)/shard_map/ppermute | solution.py:32
  (13 other events, 121.9 us)

commit v4 on v3

--- a/solution.py
+++ b/solution.py
@@ -21,7 +21,6 @@
 PIECE = SHARE + 8
 PARTS = 8
 LISTED = TMAX // PARTS
-highest = lax.Precision.HIGHEST
 f32 = jnp.float32
 bf16 = jnp.bfloat16
 together = lax.optimization_barrier
@@ -115,25 +114,25 @@
     )(index, mask, *sources)
 
 
+def product(left, right, dims):
+    left_high, left_low = split_terms(left)
+    right_high, right_low = split_terms(right)
+    dot = lambda a, b: lax.dot_general(a, b, (dims, ((), ())), preferred_element_type=f32)
+    return dot(left_high, right_high) + (dot(left_high, right_low) + dot(left_low, right_high))
+
+
 def dense_body(a_ref, b_ref, c_ref, d_ref, x_ref, w_ref, o_ref, g_ref, hidden_ref, out_ref, gw_ref):
     total = a_ref[...] + b_ref[...] + c_ref[...] + d_ref[...]
     degree = 1.0 + total[F : F + 1]
     aggregated = (total[:F] + x_ref[...]) / degree
     weight = w_ref[...]
-    active = (
-        jnp.dot(aggregated.T, weight, precision=highest, preferred_element_type=f32) + o_ref[...]
-    )
+    active = product(aggregated.T, weight, ((1,), (0,))) + o_ref[...]
     bell = 1.0 + lax.erf(active * 0.7071067811865476)
     hidden_ref[...] = 0.5 * active * bell
     slope = 0.5 * bell + active * jnp.exp(-0.5 * active * active) * 0.3989422804014327
     grad_pre = g_ref[...] * slope
-    out_ref[...] = (
-        lax.dot_general(
-            weight, grad_pre, (((1,), (1,)), ((), ())), precision=highest, preferred_element_type=f32
-        )
-        / degree
-    )
-    gw_ref[:F, :] = jnp.dot(aggregated, grad_pre, precision=highest, preferred_element_type=f32)
+    out_ref[...] = product(weight, grad_pre, ((1,), (1,))) / degree
+    gw_ref[:F, :] = product(aggregated, grad_pre, ((1,), (0,)))
     gw_ref[F:, :] = jnp.broadcast_to(jnp.sum(grad_pre, axis=0, keepdims=True), (8, H))
 
 

time: 149 us -> 148 us (level)
  no operation moved by 1% of the time
where the time goes in v4:
time: 148 us
  waiting for transfers between devices  58.2 us (39%)
  starting transfers between devices  42.5 us (29%)
  blocking collectives  35.2 us (24%)
  Pallas kernels  9 us (6%)
    ppermute x33, waiting for transfers between devices, shift(): lax.ppermute(value, axis, [(i, (i + by) % size) for i in range(size)])  58.2 us
    ppermute x33, starting transfers between devices, shift(): lax.ppermute(value, axis, [(i, (i + by) % size) for i in range(size)])  42.5 us
    all_to_all x1, blocking collectives, scatter_row(): return (lax.all_to_all(total, PLANE, 0, 0, tiled=True), piece)  20.6 us
    all_to_all x1, blocking collectives, gather_col(): lax.all_to_all(shares, PLANE, 0, 0, tiled=True)  14.5 us
    pallas_call x1, Pallas kernels, forward_products(): pl.pallas_call(forward_body, in_specs=[pl.BlockSpec(memory_space=pltpu.SM...  4.74 us
  transfers between devices with their start and end apart: 33, of which 19 were waited for; matrix products, arithmetic and copies ran while one was open for 0% of the time, Pallas kernels for 2%

profile of v4, /device:TPU:8, one launch (start us, length us, event | category | flops | bytes accessed | tf_op | source)
XLA Modules:
  0.0 147.8 jit_solution(991940726578224565)
XLA Ops:
  1.7 2.4 %collective-permute-start = (f32[128,256]{1,0:T(8,128)S(1)}, f32[128,256]{1,0:T(8,128)S(1)}, u32[]{:S(2)}, u32[]{:S(2)}) collective-permute-start(f32[128,256]{1,0:T(8,128)S(1)} %bitcast.32), channel_id=1, source_target_pairs={{0,32},{32,0},{1,33},{33,1},{2,34},{34,2},{3,35},{35,3},{4,36},{36... | collective-permute-start | bytes 393224 | tf_op jit(solution)/shard_map/ppermute | solution.py:31
  8.5 2.8 %collective-permute-start.2 = (f32[128,256]{1,0:T(8,128)S(1)}, f32[128,256]{1,0:T(8,128)S(1)}, u32[]{:S(2)}, u32[]{:S(2)}) collective-permute-start(f32[128,256]{1,0:T(8,128)S(1)} %collective-permute-done.refs_1_), channel_id=1, source_target_pairs={{0,192},{64,0},{128,64},{192,128},{1,193},{65,1},{129,65},{193,129... | collective-permute-start | bytes 393224 | tf_op jit(solution)/shard_map/ppermute | solution.py:31
  13.8 3.7 %collective-permute-start.5 = (f32[128,256]{1,0:T(8,128)S(1)}, f32[128,256]{1,0:T(8,128)S(1)}, u32[]{:S(2)}, u32[]{:S(2)}) collective-permute-start(f32[128,256]{1,0:T(8,128)S(1)} %collective-permute-done.2.refs_3_), channel_id=1, source_target_pairs={{0,192},{64,0},{128,64},{192,128},{1,193},{65,1},{129,65},{193,129... | collective-permute-start | bytes 393224 | tf_op jit(solution)/shard_map/ppermute | solution.py:31
  21.8 4.7 %shard_map.93 = (f32[16,136,256]{2,1,0:T(8,128)S(1)}, s8[32,256,256]{2,1,0:T(32,128)(4,1)S(1)}) custom-call(s32[2,32]{1,0:T(2,128)S(1)} %bitcast.38, s32[32,256,256]{2,1,0:T(8,128)} %bitcast.41, f32[128,256]{1,0:T(8,128)S(1)} %bitcast.36, f32[128,256]{1,0:T(8,128)S(1)} %collective-permute-done.refs_1_, f32[128,256]{1,0:T(8,128)S(1)} %collective-permute-done.1.refs_2_, ...), custom_call_target="tpu_custom_call" | custom-call | flops 1073741824 | bytes 4194304 | tf_op jit(solution)/shard_map/pallas_call | solution.py:98
  26.6 5.9 %collective-permute-start.15 = (f32[136,256]{1,0:T(8,128)S(1)}, f32[136,256]{1,0:T(8,128)S(1)}, u32[]{:S(2)}, u32[]{:S(2)}) collective-permute-start(f32[136,256]{1,0:T(8,128)S(1)} %get-tuple-element.76), channel_id=1, source_target_pairs={{0,14},{2,0},{4,2},{6,4},{8,6},{10,8},{12,10},{14,12},{1,15},{3,1}... | collective-permute-start | bytes 417800 | tf_op jit(solution)/shard_map/ppermute | solution.py:31
  32.7 3.1 %collective-permute-done.15 = f32[136,256]{1,0:T(8,128)S(1)} collective-permute-done((f32[136,256]{1,0:T(8,128)S(1)}, f32[136,256]{1,0:T(8,128)S(1)}, u32[]{:S(2)}, u32[]{:S(2)}) %collective-permute-start.15) | collective-permute-done | bytes 139296 | tf_op jit(solution)/shard_map/ppermute | solution.py:31
  35.8 3.4 %collective-permute-done.11 = f32[136,256]{1,0:T(8,128)S(1)} collective-permute-done((f32[136,256]{1,0:T(8,128)S(1)}, f32[136,256]{1,0:T(8,128)S(1)}, u32[]{:S(2)}, u32[]{:S(2)}) %collective-permute-start.11) | collective-permute-done | bytes 139296 | tf_op jit(solution)/shard_map/ppermute | solution.py:31
  41.5 5.5 %collective-permute-done.16 = f32[272,256]{1,0:T(8,128)S(1)} collective-permute-done((f32[272,256]{1,0:T(8,128)S(1)}, f32[272,256]{1,0:T(8,128)S(1)}, u32[]{:S(2)}, u32[]{:S(2)}) %collective-permute-start.16) | collective-permute-done | bytes 278560 | tf_op jit(solution)/shard_map/ppermute | solution.py:31
  49.3 4.6 %collective-permute-done.17 = f32[272,256]{1,0:T(8,128)S(1)} collective-permute-done((f32[272,256]{1,0:T(8,128)S(1)}, f32[272,256]{1,0:T(8,128)S(1)}, u32[]{:S(2)}, u32[]{:S(2)}) %collective-permute-start.17) | collective-permute-done | bytes 278560 | tf_op jit(solution)/shard_map/ppermute | solution.py:31
  53.9 3.3 %collective-permute-start.18 = (f32[272,256]{1,0:T(8,128)S(1)}, f32[272,256]{1,0:T(8,128)S(1)}, u32[]{:S(2)}, u32[]{:S(2)}) collective-permute-start(f32[272,256]{1,0:T(8,128)S(1)} %bitcast_add_fusion), channel_id=1, source_target_pairs={{0,14},{2,0},{4,2},{6,4},{8,6},{10,8},{12,10},{14,12},{1,15},{3,1}... | collective-permute-start | bytes 835592 | tf_op jit(solution)/shard_map/ppermute | solution.py:31
  57.3 3.9 %collective-permute-done.18 = f32[272,256]{1,0:T(8,128)S(1)} collective-permute-done((f32[272,256]{1,0:T(8,128)S(1)}, f32[272,256]{1,0:T(8,128)S(1)}, u32[]{:S(2)}, u32[]{:S(2)}) %collective-permute-start.18) | collective-permute-done | bytes 278560 | tf_op jit(solution)/shard_map/ppermute | solution.py:31
  61.2 3.8 %collective-permute-done.14 = f32[272,256]{1,0:T(8,128)S(1)} collective-permute-done((f32[272,256]{1,0:T(8,128)S(1)}, f32[272,256]{1,0:T(8,128)S(1)}, u32[]{:S(2)}, u32[]{:S(2)}) %collective-permute-start.14) | collective-permute-done | bytes 278560 | tf_op jit(solution)/shard_map/ppermute | solution.py:31
  65.8 4.4 %collective-permute-done.19.d_ref = f32[136,256]{1,0:T(8,128)S(1)} collective-permute-done((f32[136,256]{1,0:T(8,128)S(1)}, f32[136,256]{1,0:T(8,128)S(1)}, u32[]{:S(2)}, u32[]{:S(2)}) %collective-permute-start.19) | collective-permute-done | bytes 139296 | tf_op jit(solution)/shard_map/ppermute | solution.py:31
  72.8 4.5 %collective-permute-done.20 = f32[128,256]{1,0:T(8,128)S(1)} collective-permute-done((f32[128,256]{1,0:T(8,128)S(1)}, f32[128,256]{1,0:T(8,128)S(1)}, u32[]{:S(2)}, u32[]{:S(2)}) %collective-permute-start.20) | collective-permute-done | bytes 131104 | tf_op jit(solution)/shard_map/ppermute | solution.py:31
  79.5 14.5 %all_to_all.10 = f32[8,24,256]{2,1,0:T(8,128)S(1)} all-to-all(f32[8,24,256]{2,1,0:T(8,128)S(1)} %pad_maximum_fusion.7), channel_id=1, replica_groups=mesh['x'=4,'yh'=2,'core'=2,'z'=8,'yl'=2] {'x','yh'}, dimensions={0} | all-to-all | bytes 393216 | tf_op jit(solution)/shard_map/all_to_all | solution.py:247
  94.2 3.2 %collective-permute-start.25 = (f32[280,256]{1,0:T(8,128)S(1)}, f32[280,256]{1,0:T(8,128)S(1)}, u32[]{:S(2)}, u32[]{:S(2)}) collective-permute-start(f32[280,256]{1,0:T(8,128)S(1)} %get-tuple-element.90), channel_id=1, source_target_pairs={{0,14},{2,0},{4,2},{6,4},{8,6},{10,8},{12,10},{14,12},{1,15},{3,1}... | collective-permute-start | bytes 860168 | tf_op jit(solution)/shard_map/ppermute | solution.py:31
  97.4 4.6 %collective-permute-done.24.refs_3_ = f32[280,256]{1,0:T(8,128)S(1)} collective-permute-done((f32[280,256]{1,0:T(8,128)S(1)}, f32[280,256]{1,0:T(8,128)S(1)}, u32[]{:S(2)}, u32[]{:S(2)}) %collective-permute-start.24) | collective-permute-done | bytes 286752 | tf_op jit(solution)/shard_map/ppermute | solution.py:31
  102.0 3.2 %collective-permute-start.27 = (f32[280,256]{1,0:T(8,128)S(1)}, f32[280,256]{1,0:T(8,128)S(1)}, u32[]{:S(2)}, u32[]{:S(2)}) collective-permute-start(f32[280,256]{1,0:T(8,128)S(1)} %collective-permute-done.25.refs_4_), channel_id=1, source_target_pairs={{0,14},{2,0},{4,2},{6,4},{8,6},{10,8},{12,10},{14,12},{1,15},{3,1}... | collective-permute-start | bytes 860168 | tf_op jit(solution)/shard_map/ppermute | solution.py:31
  105.3 5.2 %collective-permute-done.26.refs_5_ = f32[280,256]{1,0:T(8,128)S(1)} collective-permute-done((f32[280,256]{1,0:T(8,128)S(1)}, f32[280,256]{1,0:T(8,128)S(1)}, u32[]{:S(2)}, u32[]{:S(2)}) %collective-permute-start.26) | collective-permute-done | bytes 286752 | tf_op jit(solution)/shard_map/ppermute | solution.py:31
  110.6 3.5 %collective-permute-start.29 = (f32[152,256]{1,0:T(8,128)S(1)}, f32[152,256]{1,0:T(8,128)S(1)}, u32[]{:S(2)}, u32[]{:S(2)}) collective-permute-start(f32[152,256]{1,0:T(8,128)S(1)} %slice.192), channel_id=1, source_target_pairs={{0,14},{2,0},{4,2},{6,4},{8,6},{10,8},{12,10},{14,12},{1,15},{3,1}... | collective-permute-start | bytes 466952 | tf_op jit(solution)/shard_map/ppermute | solution.py:31
  114.1 3.0 %collective-permute-done.28.refs_7_ = f32[152,256]{1,0:T(8,128)S(1)} collective-permute-done((f32[152,256]{1,0:T(8,128)S(1)}, f32[152,256]{1,0:T(8,128)S(1)}, u32[]{:S(2)}, u32[]{:S(2)}) %collective-permute-start.28) | collective-permute-done | bytes 155680 | tf_op jit(solution)/shard_map/ppermute | solution.py:31
  119.4 2.7 %collective-permute-done.30 = f32[24,256]{1,0:T(8,128)S(1)} collective-permute-done((f32[24,256]{1,0:T(8,128)S(1)}, f32[24,256]{1,0:T(8,128)S(1)}, u32[]{:S(2)}, u32[]{:S(2)}) %collective-permute-start.30) | collective-permute-done | bytes 24608 | tf_op jit(solution)/shard_map/ppermute | solution.py:31
  123.6 2.4 %collective-permute-done.32 = f32[24,256]{1,0:T(8,128)S(1)} collective-permute-done((f32[24,256]{1,0:T(8,128)S(1)}, f32[24,256]{1,0:T(8,128)S(1)}, u32[]{:S(2)}, u32[]{:S(2)}) %collective-permute-start.32) | collective-permute-done | bytes 24608 | tf_op jit(solution)/shard_map/ppermute | solution.py:31
  126.4 20.6 %all_to_all.11.parts_ref = f32[8,144,256]{2,1,0:T(8,128)S(1)} all-to-all(f32[8,144,256]{2,1,0:T(8,128)S(1)} %pad_maximum_fusion), channel_id=1, replica_groups=mesh['x'=4,'yh'=2,'core'=2,'z'=8,'yl'=2] {'x','yh'}, dimensions={0} | all-to-all | bytes 2359296 | tf_op jit(solution)/shard_map/all_to_all | solution.py:267
  (93 shorter events, 27.8 us)
Async XLA Ops:
  1.7 6.8 %collective-permute-start = (f32[128,256]{1,0:T(8,128)S(1)}, f32[128,256]{1,0:T(8,128)S(1)}, u32[]{:S(2)}, u32[]{:S(2)}) collective-permute-start(f32[128,256]{1,0:T(8,128)S(1)} %bitcast.32), channel_id=1, source_target_pairs={{0,32},{32,0},{1,33},{33,1},{2,34},{34,2},{3,35},{35,3},{4,36},{36... | collective-permute-start | bytes 393224 | tf_op jit(solution)/shard_map/ppermute | solution.py:31
  4.0 7.2 %collective-permute-start.3 = (f32[128,256]{1,0:T(8,128)S(1)}, f32[128,256]{1,0:T(8,128)S(1)}, u32[]{:S(2)}, u32[]{:S(2)}) collective-permute-start(f32[128,256]{1,0:T(8,128)S(1)} %bitcast.33), channel_id=1, source_target_pairs={{0,64},{64,128},{128,192},{192,0},{1,65},{65,129},{129,193},{193,1... | collective-permute-start | bytes 393224 | tf_op jit(solution)/shard_map/ppermute | solution.py:31
  5.5 5.7 %collective-permute-start.1 = (f32[128,256]{1,0:T(8,128)S(1)}, f32[128,256]{1,0:T(8,128)S(1)}, u32[]{:S(2)}, u32[]{:S(2)}) collective-permute-start(f32[128,256]{1,0:T(8,128)S(1)} %bitcast.34), channel_id=1, source_target_pairs={{0,192},{64,0},{128,64},{192,128},{1,193},{65,1},{129,65},{193,129... | collective-permute-start | bytes 393224 | tf_op jit(solution)/shard_map/ppermute | solution.py:31
  11.2 7.5 %collective-permute-start.6 = (f32[128,256]{1,0:T(8,128)S(1)}, f32[128,256]{1,0:T(8,128)S(1)}, u32[]{:S(2)}, u32[]{:S(2)}) collective-permute-start(f32[128,256]{1,0:T(8,128)S(1)} %collective-permute-done.refs_1_), channel_id=1, source_target_pairs={{0,64},{64,128},{128,192},{192,0},{1,65},{65,129},{129,193},{193,1... | collective-permute-start | bytes 393224 | tf_op jit(solution)/shard_map/ppermute | solution.py:31
  11.3 9.0 %collective-permute-start.8 = (f32[256,256]{1,0:T(8,128)S(1)}, f32[256,256]{1,0:T(8,128)S(1)}, u32[]{:S(2)}, u32[]{:S(2)}) collective-permute-start(f32[256,256]{1,0:T(8,128)S(1)} %pad_maximum_fusion.4), channel_id=1, source_target_pairs={{0,16},{16,0},{1,17},{17,1},{2,18},{18,2},{3,19},{19,3},{4,20},{20... | collective-permute-start | bytes 786440 | tf_op jit(solution)/shard_map/ppermute | solution.py:31
  11.4 8.8 %collective-permute-start.4 = (f32[128,256]{1,0:T(8,128)S(1)}, f32[128,256]{1,0:T(8,128)S(1)}, u32[]{:S(2)}, u32[]{:S(2)}) collective-permute-start(f32[128,256]{1,0:T(8,128)S(1)} %collective-permute-done.3.refs_6_), channel_id=1, source_target_pairs={{0,64},{64,128},{128,192},{192,0},{1,65},{65,129},{129,193},{193,1... | collective-permute-start | bytes 393224 | tf_op jit(solution)/shard_map/ppermute | solution.py:31
  13.8 6.4 %collective-permute-start.5 = (f32[128,256]{1,0:T(8,128)S(1)}, f32[128,256]{1,0:T(8,128)S(1)}, u32[]{:S(2)}, u32[]{:S(2)}) collective-permute-start(f32[128,256]{1,0:T(8,128)S(1)} %collective-permute-done.2.refs_3_), channel_id=1, source_target_pairs={{0,192},{64,0},{128,64},{192,128},{1,193},{65,1},{129,65},{193,129... | collective-permute-start | bytes 393224 | tf_op jit(solution)/shard_map/ppermute | solution.py:31
  26.6 9.1 %collective-permute-start.15 = (f32[136,256]{1,0:T(8,128)S(1)}, f32[136,256]{1,0:T(8,128)S(1)}, u32[]{:S(2)}, u32[]{:S(2)}) collective-permute-start(f32[136,256]{1,0:T(8,128)S(1)} %get-tuple-element.76), channel_id=1, source_target_pairs={{0,14},{2,0},{4,2},{6,4},{8,6},{10,8},{12,10},{14,12},{1,15},{3,1}... | collective-permute-start | bytes 417800 | tf_op jit(solution)/shard_map/ppermute | solution.py:31
  32.6 6.6 %collective-permute-start.11 = (f32[136,256]{1,0:T(8,128)S(1)}, f32[136,256]{1,0:T(8,128)S(1)}, u32[]{:S(2)}, u32[]{:S(2)}) collective-permute-start(f32[136,256]{1,0:T(8,128)S(1)} %get-tuple-element.77), channel_id=1, source_target_pairs={{0,2},{2,4},{4,6},{6,8},{8,10},{10,12},{12,14},{14,0},{1,3},{3,5},... | collective-permute-start | bytes 417800 | tf_op jit(solution)/shard_map/ppermute | solution.py:31
  39.2 7.8 %collective-permute-start.16 = (f32[272,256]{1,0:T(8,128)S(1)}, f32[272,256]{1,0:T(8,128)S(1)}, u32[]{:S(2)}, u32[]{:S(2)}) collective-permute-start(f32[272,256]{1,0:T(8,128)S(1)} %get-tuple-element.74), channel_id=1, source_target_pairs={{0,14},{2,0},{4,2},{6,4},{8,6},{10,8},{12,10},{14,12},{1,15},{3,1}... | collective-permute-start | bytes 835592 | tf_op jit(solution)/shard_map/ppermute | solution.py:31
  39.8 9.2 %collective-permute-start.12 = (f32[272,256]{1,0:T(8,128)S(1)}, f32[272,256]{1,0:T(8,128)S(1)}, u32[]{:S(2)}, u32[]{:S(2)}) collective-permute-start(f32[272,256]{1,0:T(8,128)S(1)} %get-tuple-element.75), channel_id=1, source_target_pairs={{0,2},{2,4},{4,6},{6,8},{8,10},{10,12},{12,14},{14,0},{1,3},{3,5},... | collective-permute-start | bytes 835592 | tf_op jit(solution)/shard_map/ppermute | solution.py:31
  47.0 6.8 %collective-permute-start.17 = (f32[272,256]{1,0:T(8,128)S(1)}, f32[272,256]{1,0:T(8,128)S(1)}, u32[]{:S(2)}, u32[]{:S(2)}) collective-permute-start(f32[272,256]{1,0:T(8,128)S(1)} %bitcast_add_fusion.1), channel_id=1, source_target_pairs={{0,14},{2,0},{4,2},{6,4},{8,6},{10,8},{12,10},{14,12},{1,15},{3,1}... | collective-permute-start | bytes 835592 | tf_op jit(solution)/shard_map/ppermute | solution.py:31
  49.0 8.2 %collective-permute-start.13 = (f32[272,256]{1,0:T(8,128)S(1)}, f32[272,256]{1,0:T(8,128)S(1)}, u32[]{:S(2)}, u32[]{:S(2)}) collective-permute-start(f32[272,256]{1,0:T(8,128)S(1)} %bitcast_add_fusion.3), channel_id=1, source_target_pairs={{0,2},{2,4},{4,6},{6,8},{8,10},{10,12},{12,14},{14,0},{1,3},{3,5},... | collective-permute-start | bytes 835592 | tf_op jit(solution)/shard_map/ppermute | solution.py:31
  53.9 7.3 %collective-permute-start.18 = (f32[272,256]{1,0:T(8,128)S(1)}, f32[272,256]{1,0:T(8,128)S(1)}, u32[]{:S(2)}, u32[]{:S(2)}) collective-permute-start(f32[272,256]{1,0:T(8,128)S(1)} %bitcast_add_fusion), channel_id=1, source_target_pairs={{0,14},{2,0},{4,2},{6,4},{8,6},{10,8},{12,10},{14,12},{1,15},{3,1}... | collective-permute-start | bytes 835592 | tf_op jit(solution)/shard_map/ppermute | solution.py:31
  57.2 7.8 %collective-permute-start.14 = (f32[272,256]{1,0:T(8,128)S(1)}, f32[272,256]{1,0:T(8,128)S(1)}, u32[]{:S(2)}, u32[]{:S(2)}) collective-permute-start(f32[272,256]{1,0:T(8,128)S(1)} %bitcast_add_fusion.2), channel_id=1, source_target_pairs={{0,2},{2,4},{4,6},{6,8},{8,10},{10,12},{12,14},{14,0},{1,3},{3,5},... | collective-permute-start | bytes 835592 | tf_op jit(solution)/shard_map/ppermute | solution.py:31
  71.4 5.9 %collective-permute-start.20 = (f32[128,256]{1,0:T(8,128)S(1)}, f32[128,256]{1,0:T(8,128)S(1)}, u32[]{:S(2)}, u32[]{:S(2)}) collective-permute-start(f32[128,256]{1,0:T(8,128)S(1)} %get-tuple-element.51.out_ref), channel_id=1, source_target_pairs={{0,1},{1,0},{2,3},{3,2},{4,5},{5,4},{6,7},{7,6},{8,9},{9,8},{10,11... | collective-permute-start | bytes 393224 | tf_op jit(solution)/shard_map/ppermute | solution.py:31
  77.4 16.7 %collective-permute-start.23 = (f32[256,256]{1,0:T(8,128)S(1)}, f32[256,256]{1,0:T(8,128)S(1)}, u32[]{:S(2)}, u32[]{:S(2)}) collective-permute-start(f32[256,256]{1,0:T(8,128)S(1)} %constant_dynamic-update-slice_fusion.refs_0_), channel_id=1, source_target_pairs={{0,14},{2,0},{4,2},{6,4},{8,6},{10,8},{12,10},{14,12},{1,15},{3,1}... | collective-permute-start | bytes 786440 | tf_op jit(solution)/shard_map/ppermute | solution.py:31
  77.4 16.6 %collective-permute-start.22 = (f32[256,256]{1,0:T(8,128)S(1)}, f32[256,256]{1,0:T(8,128)S(1)}, u32[]{:S(2)}, u32[]{:S(2)}) collective-permute-start(f32[256,256]{1,0:T(8,128)S(1)} %constant_dynamic-update-slice_fusion.refs_0_), channel_id=1, source_target_pairs={{0,2},{2,4},{4,6},{6,8},{8,10},{10,12},{12,14},{14,0},{1,3},{3,5},... | collective-permute-start | bytes 786440 | tf_op jit(solution)/shard_map/ppermute | solution.py:31
  94.1 7.9 %collective-permute-start.24 = (f32[280,256]{1,0:T(8,128)S(1)}, f32[280,256]{1,0:T(8,128)S(1)}, u32[]{:S(2)}, u32[]{:S(2)}) collective-permute-start(f32[280,256]{1,0:T(8,128)S(1)} %get-tuple-element.91), channel_id=1, source_target_pairs={{0,2},{2,4},{4,6},{6,8},{8,10},{10,12},{12,14},{14,0},{1,3},{3,5},... | collective-permute-start | bytes 860168 | tf_op jit(solution)/shard_map/ppermute | solution.py:31
  94.2 7.8 %collective-permute-start.25 = (f32[280,256]{1,0:T(8,128)S(1)}, f32[280,256]{1,0:T(8,128)S(1)}, u32[]{:S(2)}, u32[]{:S(2)}) collective-permute-start(f32[280,256]{1,0:T(8,128)S(1)} %get-tuple-element.90), channel_id=1, source_target_pairs={{0,14},{2,0},{4,2},{6,4},{8,6},{10,8},{12,10},{14,12},{1,15},{3,1}... | collective-permute-start | bytes 860168 | tf_op jit(solution)/shard_map/ppermute | solution.py:31
  102.0 8.4 %collective-permute-start.26 = (f32[280,256]{1,0:T(8,128)S(1)}, f32[280,256]{1,0:T(8,128)S(1)}, u32[]{:S(2)}, u32[]{:S(2)}) collective-permute-start(f32[280,256]{1,0:T(8,128)S(1)} %collective-permute-done.24.refs_3_), channel_id=1, source_target_pairs={{0,2},{2,4},{4,6},{6,8},{8,10},{10,12},{12,14},{14,0},{1,3},{3,5},... | collective-permute-start | bytes 860168 | tf_op jit(solution)/shard_map/ppermute | solution.py:31
  102.0 8.5 %collective-permute-start.27 = (f32[280,256]{1,0:T(8,128)S(1)}, f32[280,256]{1,0:T(8,128)S(1)}, u32[]{:S(2)}, u32[]{:S(2)}) collective-permute-start(f32[280,256]{1,0:T(8,128)S(1)} %collective-permute-done.25.refs_4_), channel_id=1, source_target_pairs={{0,14},{2,0},{4,2},{6,4},{8,6},{10,8},{12,10},{14,12},{1,15},{3,1}... | collective-permute-start | bytes 860168 | tf_op jit(solution)/shard_map/ppermute | solution.py:31
  110.5 6.6 %collective-permute-start.28 = (f32[152,256]{1,0:T(8,128)S(1)}, f32[152,256]{1,0:T(8,128)S(1)}, u32[]{:S(2)}, u32[]{:S(2)}) collective-permute-start(f32[152,256]{1,0:T(8,128)S(1)} %pad_maximum_fusion.8), channel_id=1, source_target_pairs={{0,2},{2,4},{4,6},{6,8},{8,10},{10,12},{12,14},{14,0},{1,3},{3,5},... | collective-permute-start | bytes 466952 | tf_op jit(solution)/shard_map/ppermute | solution.py:31
  110.6 6.5 %collective-permute-start.29 = (f32[152,256]{1,0:T(8,128)S(1)}, f32[152,256]{1,0:T(8,128)S(1)}, u32[]{:S(2)}, u32[]{:S(2)}) collective-permute-start(f32[152,256]{1,0:T(8,128)S(1)} %slice.192), channel_id=1, source_target_pairs={{0,14},{2,0},{4,2},{6,4},{8,6},{10,8},{12,10},{14,12},{1,15},{3,1}... | collective-permute-start | bytes 466952 | tf_op jit(solution)/shard_map/ppermute | solution.py:31
  (13 other events, 121.8 us)
